TPU v7x, 32 devices: a whole 2x2x4 slice. The times are simulated.
32 devices in a mesh: dev: 32 (over z, y, x, core).
Axes of the slice: x: 2, y: 2, z: 4, core: 2. Of those that a mesh axis runs over, the one named last changes fastest.
Arguments:
- tokens: bfloat16 [12288, 1024], P('dev'), may hold values from -6 to 6
- cotangent: bfloat16 [12288, 1024], P('dev'), may hold values from -6 to 6
- image_lengths: int32 [12], replicated, may hold values from 1 to 1370, 12288 in all
- ln1_gain: bfloat16 [1024], P('dev'), may hold values from 0.5 to 1.5
- ln1_bias: bfloat16 [1024], P('dev'), may hold values from -1.75 to 1.75
- qkv_weight: bfloat16 [1024, 3072], P('dev'), may hold values from -0.1875 to 0.1875
- qv_bias: bfloat16 [2048], P('dev'), may hold values from -1.75 to 1.75
- proj_weight: bfloat16 [1024, 1024], P('dev'), may hold values from -1 to 1
- proj_bias: bfloat16 [1024], P('dev'), may hold values from -1.75 to 1.75
- scale_attn: bfloat16 [1024], P('dev'), may hold values from 0.5 to 2
- ln2_gain: bfloat16 [1024], P('dev'), may hold values from 0.5 to 1.5
- ln2_bias: bfloat16 [1024], P('dev'), may hold values from -1.75 to 1.75
- fc1_weight: bfloat16 [1024, 4096], P('dev'), may hold values from -0.1875 to 0.1875
- fc1_bias: bfloat16 [4096], P('dev'), may hold values from -1.75 to 1.75
- fc2_weight: bfloat16 [4096, 1024], P('dev'), may hold values from -0.09375 to 0.09375
- fc2_bias: bfloat16 [1024], P('dev'), may hold values from -1.75 to 1.75
- scale_mlp: bfloat16 [1024], P('dev'), may hold values from 0.5 to 2
Outputs:
- block_out: bfloat16 [12288, 1024], P('dev')
- grad_tokens: bfloat16 [12288, 1024], P('dev')
- grad_ln1_gain: float32 [1024], P('dev')
- grad_ln1_bias: float32 [1024], P('dev')
- grad_qkv_weight: float32 [1024, 3072], P('dev')
- grad_qv_bias: float32 [2048], P('dev')
- grad_proj_weight: float32 [1024, 1024], P('dev')
- grad_proj_bias: float32 [1024], P('dev')
- grad_scale_attn: float32 [1024], P('dev')
- grad_ln2_gain: float32 [1024], P('dev')
- grad_ln2_bias: float32 [1024], P('dev')
- grad_fc1_weight: float32 [1024, 4096], P('dev')
- grad_fc1_bias: float32 [4096], P('dev')
- grad_fc2_weight: float32 [4096, 1024], P('dev')
- grad_fc2_bias: float32 [1024], P('dev')
- grad_scale_mlp: float32 [1024], P('dev')
Inputs may be any that keep to these rules, and one draw needn't show every extreme that they name: `image_lengths`: they sum to 12288; the longest image has exactly 1370 tokens.
All inputs are finite; a program needn't handle non-finite values.
Results may differ from a plain program's by a relative error of at most 0.011.
Values may be sent and summed in bfloat16 or wider, within the bound.
No kernel may reach another device: no remote copies, remote signals or barrier semaphores. Data moves between devices by JAX's collectives and lax.ppermute only.
A program may use at most 192 MiB of HBM per device.

v0:
```python
import jax
import jax.numpy as jnp
from jax import lax
from jax.sharding import PartitionSpec as P

HEADS = 16
SEQ = 1370


eps = 1e-06


def shifted(shard, axis, by):
    devices = lax.axis_size(axis)
    pairs = [(i, i + by) for i in range(devices) if 0 <= i + by < devices]
    return lax.ppermute(shard, axis, pairs)


def layer_norm(value, gain, shift):
    centre = value - jnp.mean(value, axis=-1, keepdims=True)
    spread = jnp.mean(centre * centre, axis=-1, keepdims=True)
    return centre * lax.rsqrt(spread + eps) * gain + shift


def gelu_exact(value):
    return jax.nn.gelu(value, approximate=False)


def split_heads(matrix, heads):
    return matrix.reshape(matrix.shape[0], heads, -1).transpose(1, 0, 2)


def join_heads(stacked):
    return stacked.transpose(1, 0, 2).reshape(stacked.shape[1], -1)


def body(
    tokens,
    cotangent,
    image_lengths,
    ln1_gain,
    ln1_bias,
    qkv_weight,
    qv_bias,
    proj_weight,
    proj_bias,
    scale_attn,
    ln2_gain,
    ln2_bias,
    fc1_weight,
    fc1_bias,
    fc2_weight,
    fc2_bias,
    scale_mlp,
):
    gathered = (
        lax.all_gather(ln1_gain, "dev", axis=0, tiled=True),
        lax.all_gather(ln1_bias, "dev", axis=0, tiled=True),
        lax.all_gather(qkv_weight, "dev", axis=0, tiled=True),
        lax.all_gather(qv_bias, "dev", axis=0, tiled=True),
        lax.all_gather(proj_weight, "dev", axis=0, tiled=True),
        lax.all_gather(proj_bias, "dev", axis=0, tiled=True),
        lax.all_gather(scale_attn, "dev", axis=0, tiled=True),
        lax.all_gather(ln2_gain, "dev", axis=0, tiled=True),
        lax.all_gather(ln2_bias, "dev", axis=0, tiled=True),
        lax.all_gather(fc1_weight, "dev", axis=0, tiled=True),
        lax.all_gather(fc1_bias, "dev", axis=0, tiled=True),
        lax.all_gather(fc2_weight, "dev", axis=0, tiled=True),
        lax.all_gather(fc2_bias, "dev", axis=0, tiled=True),
        lax.all_gather(scale_mlp, "dev", axis=0, tiled=True),
    )
    (
        gain_one,
        shift_one,
        w_qkv,
        bias_qv,
        w_proj,
        bias_proj,
        layer_attn,
        gain_two,
        shift_two,
        w_fc1,
        bias_fc1,
        w_fc2,
        bias_fc2,
        layer_mlp,
    ) = gathered
    rows, width = tokens.shape
    heads = HEADS
    reach = (SEQ + rows - 2) // rows
    shard = lax.axis_index("dev")
    total_rows = rows * lax.axis_size("dev")
    ends = jnp.cumsum(image_lengths)

    def image_ids(first, count):
        places = first + jnp.arange(count, dtype=jnp.int32)
        inside = (places >= 0) & (places < total_rows)
        ids = jnp.sum((places[:, None] >= ends[None, :]).astype(jnp.int32), axis=1)
        return jnp.where(inside, ids, -1)

    own_ids = image_ids(shard * rows, rows)
    window_ids = image_ids((shard - reach) * rows, (2 * reach + 1) * rows)
    same = own_ids[:, None] == window_ids[None, :]
    x_full = tokens.astype(jnp.float32)
    norm_one = layer_norm(x_full, gain_one.astype(jnp.float32), shift_one.astype(jnp.float32))
    norm_one_low = norm_one.astype(jnp.bfloat16)
    qkv = jnp.dot(norm_one_low, w_qkv, preferred_element_type=jnp.float32)
    bias_both = bias_qv.astype(jnp.float32)
    query = (qkv[:, :width] + bias_both[:width]).astype(jnp.bfloat16)
    key = qkv[:, width : 2 * width].astype(jnp.bfloat16)
    value = (qkv[:, 2 * width :] + bias_both[width:]).astype(jnp.bfloat16)
    key_value = jnp.concatenate([key, value], axis=1)
    pieces = []
    for offset in range(-reach, reach + 1):
        if offset == 0:
            pieces.append(key_value)
        else:
            pieces.append(shifted(key_value, "dev", -offset))
    window = jnp.concatenate(pieces, axis=0)
    q_heads = split_heads(query, heads)
    k_heads = split_heads(window[:, :width], heads)
    v_heads = split_heads(window[:, width:], heads)

    def head_forward(parts):
        q_one, k_one, v_one = parts
        scores = jnp.einsum("qd,kd->qk", q_one, k_one, preferred_element_type=jnp.float32) * 0.125
        scores = jnp.where(same, scores, -1e30)
        top = jnp.max(scores, axis=1, keepdims=True)
        expo = jnp.exp(scores - top)
        summed = jnp.sum(expo, axis=1, keepdims=True)
        prob = (expo / summed).astype(jnp.bfloat16)
        out = jnp.dot(prob, v_one, preferred_element_type=jnp.float32)
        return (out, (top + jnp.log(summed))[:, 0])

    attn_heads, log_totals = lax.map(head_forward, (q_heads, k_heads, v_heads))
    mixed_low = join_heads(attn_heads).astype(jnp.bfloat16)
    branch = jnp.dot(mixed_low, w_proj, preferred_element_type=jnp.float32) + bias_proj.astype(
        jnp.float32
    )
    hidden = x_full + layer_attn.astype(jnp.float32) * branch
    norm_two = layer_norm(hidden, gain_two.astype(jnp.float32), shift_two.astype(jnp.float32))
    norm_two_low = norm_two.astype(jnp.bfloat16)
    pre = jnp.dot(norm_two_low, w_fc1, preferred_element_type=jnp.float32) + bias_fc1.astype(
        jnp.float32
    )
    act_low = gelu_exact(pre).astype(jnp.bfloat16)
    mlp = jnp.dot(act_low, w_fc2, preferred_element_type=jnp.float32) + bias_fc2.astype(jnp.float32)
    block_out = (hidden + layer_mlp.astype(jnp.float32) * mlp).astype(jnp.bfloat16)
    again = (
        lax.all_gather(ln1_gain, "dev", axis=0, tiled=True),
        lax.all_gather(ln1_bias, "dev", axis=0, tiled=True),
        lax.all_gather(qkv_weight, "dev", axis=0, tiled=True),
        lax.all_gather(qv_bias, "dev", axis=0, tiled=True),
        lax.all_gather(proj_weight, "dev", axis=0, tiled=True),
        lax.all_gather(proj_bias, "dev", axis=0, tiled=True),
        lax.all_gather(scale_attn, "dev", axis=0, tiled=True),
        lax.all_gather(ln2_gain, "dev", axis=0, tiled=True),
        lax.all_gather(ln2_bias, "dev", axis=0, tiled=True),
        lax.all_gather(fc1_weight, "dev", axis=0, tiled=True),
        lax.all_gather(fc1_bias, "dev", axis=0, tiled=True),
        lax.all_gather(fc2_weight, "dev", axis=0, tiled=True),
        lax.all_gather(fc2_bias, "dev", axis=0, tiled=True),
        lax.all_gather(scale_mlp, "dev", axis=0, tiled=True),
    )
    (
        back_gain_one,
        back_shift_one,
        back_qkv,
        unused_bias,
        back_proj,
        unused_proj_bias,
        back_attn_scale,
        back_gain_two,
        back_shift_two,
        back_fc1,
        unused_fc1_bias,
        back_fc2,
        unused_fc2_bias,
        back_mlp_scale,
    ) = again
    grad_out = cotangent.astype(jnp.float32)
    d_scale_mlp = jnp.sum(grad_out * mlp, axis=0)
    d_mlp = grad_out * back_mlp_scale.astype(jnp.float32)
    d_fc2_bias = jnp.sum(d_mlp, axis=0)
    d_mlp_low = d_mlp.astype(jnp.bfloat16)
    d_fc2 = jnp.einsum("tf,td->fd", act_low, d_mlp_low, preferred_element_type=jnp.float32)
    d_act = jnp.einsum("td,fd->tf", d_mlp_low, back_fc2, preferred_element_type=jnp.float32)
    unused_act, gelu_pull = jax.vjp(gelu_exact, pre)
    d_pre = gelu_pull(d_act)[0]
    d_fc1_bias = jnp.sum(d_pre, axis=0)
    d_pre_low = d_pre.astype(jnp.bfloat16)
    d_fc1 = jnp.einsum("td,tf->df", norm_two_low, d_pre_low, preferred_element_type=jnp.float32)
    d_norm_two = jnp.einsum("tf,df->td", d_pre_low, back_fc1, preferred_element_type=jnp.float32)
    unused_two, norm_two_pull = jax.vjp(
        layer_norm, hidden, back_gain_two.astype(jnp.float32), back_shift_two.astype(jnp.float32)
    )
    d_hidden_norm, d_gain_two, d_shift_two = norm_two_pull(d_norm_two)
    d_hidden = grad_out + d_hidden_norm
    d_scale_attn = jnp.sum(d_hidden * branch, axis=0)
    d_branch = d_hidden * back_attn_scale.astype(jnp.float32)
    d_proj_bias = jnp.sum(d_branch, axis=0)
    d_branch_low = d_branch.astype(jnp.bfloat16)
    d_proj = jnp.einsum("td,te->de", mixed_low, d_branch_low, preferred_element_type=jnp.float32)
    d_mixed = jnp.einsum(
        "te,de->td", d_branch_low, back_proj, preferred_element_type=jnp.float32
    ).astype(jnp.bfloat16)
    d_heads = split_heads(d_mixed, heads)

    def head_backward(parts):
        q_one, k_one, v_one, d_one, log_one = parts
        scores = jnp.einsum("qd,kd->qk", q_one, k_one, preferred_element_type=jnp.float32) * 0.125
        prob = jnp.where(same, jnp.exp(scores - log_one[:, None]), 0.0)
        d_prob = jnp.einsum("qd,kd->qk", d_one, v_one, preferred_element_type=jnp.float32)
        d_val = jnp.einsum(
            "qk,qd->kd", prob.astype(jnp.bfloat16), d_one, preferred_element_type=jnp.float32
        )
        centre = jnp.sum(prob * d_prob, axis=1, keepdims=True)
        d_scores = (prob * (d_prob - centre)).astype(jnp.bfloat16)
        d_que = jnp.einsum("qk,kd->qd", d_scores, k_one, preferred_element_type=jnp.float32) * 0.125
        d_key = jnp.einsum("qk,qd->kd", d_scores, q_one, preferred_element_type=jnp.float32) * 0.125
        return (d_que, d_key, d_val)

    d_query_heads, d_key_heads, d_value_heads = lax.map(
        head_backward, (q_heads, k_heads, v_heads, d_heads, log_totals)
    )
    d_window = jnp.concatenate([join_heads(d_key_heads), join_heads(d_value_heads)], axis=1)
    d_pair = jnp.zeros((rows, 2 * width), jnp.float32)
    for offset in range(-reach, reach + 1):
        piece = d_window[(offset + reach) * rows : (offset + reach + 1) * rows]
        if offset == 0:
            d_pair = d_pair + piece
        else:
            d_pair = d_pair + shifted(piece.astype(jnp.bfloat16), "dev", offset).astype(piece.dtype)
    d_query_low = join_heads(d_query_heads).astype(jnp.bfloat16)
    d_pair_low = d_pair.astype(jnp.bfloat16)
    d_qv_bias = jnp.concatenate(
        [
            jnp.sum(d_query_low.astype(jnp.float32), axis=0),
            jnp.sum(d_pair_low[:, width:].astype(jnp.float32), axis=0),
        ]
    )
    d_qkv = jnp.concatenate([d_query_low, d_pair_low], axis=1)
    d_qkv_weight = jnp.einsum("td,te->de", norm_one_low, d_qkv, preferred_element_type=jnp.float32)
    d_norm_one = jnp.einsum("te,de->td", d_qkv, back_qkv, preferred_element_type=jnp.float32)
    unused_one, norm_one_pull = jax.vjp(
        layer_norm, x_full, back_gain_one.astype(jnp.float32), back_shift_one.astype(jnp.float32)
    )
    d_input_norm, d_gain_one, d_shift_one = norm_one_pull(d_norm_one)
    grad_tokens = (d_hidden + d_input_norm).astype(jnp.bfloat16)
    shares = (
        lax.psum_scatter(d_gain_one, "dev", scatter_dimension=0, tiled=True),
        lax.psum_scatter(d_shift_one, "dev", scatter_dimension=0, tiled=True),
        lax.psum_scatter(d_qkv_weight, "dev", scatter_dimension=0, tiled=True),
        lax.psum_scatter(d_qv_bias, "dev", scatter_dimension=0, tiled=True),
        lax.psum_scatter(d_proj, "dev", scatter_dimension=0, tiled=True),
        lax.psum_scatter(d_proj_bias, "dev", scatter_dimension=0, tiled=True),
        lax.psum_scatter(d_scale_attn, "dev", scatter_dimension=0, tiled=True),
        lax.psum_scatter(d_gain_two, "dev", scatter_dimension=0, tiled=True),
        lax.psum_scatter(d_shift_two, "dev", scatter_dimension=0, tiled=True),
        lax.psum_scatter(d_fc1, "dev", scatter_dimension=0, tiled=True),
        lax.psum_scatter(d_fc1_bias, "dev", scatter_dimension=0, tiled=True),
        lax.psum_scatter(d_fc2, "dev", scatter_dimension=0, tiled=True),
        lax.psum_scatter(d_fc2_bias, "dev", scatter_dimension=0, tiled=True),
        lax.psum_scatter(d_scale_mlp, "dev", scatter_dimension=0, tiled=True),
    )
    return (
        block_out,
        grad_tokens,
        shares[0],
        shares[1],
        shares[2],
        shares[3],
        shares[4],
        shares[5],
        shares[6],
        shares[7],
        shares[8],
        shares[9],
        shares[10],
        shares[11],
        shares[12],
        shares[13],
    )


def solution(mesh):
    placed = (
        P("dev", None),
        P("dev", None),
        P(),
        P("dev"),
        P("dev"),
        P("dev", None),
        P("dev"),
        P("dev", None),
        P("dev"),
        P("dev"),
        P("dev"),
        P("dev"),
        P("dev", None),
        P("dev"),
        P("dev", None),
        P("dev"),
        P("dev"),
    )
    return jax.shard_map(
        body,
        mesh=mesh,
        in_specs=placed,
        out_specs=(
            P("dev", None),
            P("dev", None),
            P("dev"),
            P("dev"),
            P("dev", None),
            P("dev"),
            P("dev", None),
            P("dev"),
            P("dev"),
            P("dev"),
            P("dev"),
            P("dev", None),
            P("dev"),
            P("dev", None),
            P("dev"),
            P("dev"),
        ),
        check_vma=False,
    )
```

profile of v0, /device:TPU:0, one launch (start us, length us, event | category | flops | bytes accessed | tf_op | source)
XLA Modules:
  0.0 1662.5 jit_solution(10886220029667337503)
XLA Ops:
  17.0 42.6 %all-reduce.20 = (bf16[1024]{0:T(1024)(128)(2,1)S(1)}, bf16[1024]{0:T(1024)(128)(2,1)S(1)}, bf16[2048]{0:T(1024)(128)(2,1)S(1)}, bf16[1024]{0:T(1024)(128)(2,1)S...) all-reduce(bf16[1024]{0:T(1024)(128)(2,1)S(1)} %dynamic-update-slic, ...), channel_id=1, replica_groups=mesh['dev'=32] {'dev'}, use_global_device_ids=true, to_apply=%add.2 | all-reduce | flops 10240 | bytes 40960
  63.0 20.3 %all-gather.6.cloned.1.call-done = bf16[1024,3072]{1,0:T(8,128)(2,1)} async-done(((bf16[32,3072]{1,0:T(8,128)(2,1)}), bf16[1024,3072]{1,0:T(8,128)(2,1)}) %all-gather.6.cloned.1.call-update) | async-done | bytes 6291472 | tf_op jit(solution)/shard_map/all_gather | solution.py:59
  83.3 5.1 fusion.95
  90.3 4.5 collective-permute-start
  98.2 4.3 collective-permute-start.2
  106.8 154.6 %all-gather = bf16[32,1,128]{2,1,0:T(2,128)(2,1)S(1)} all-gather(bf16[1,1,128]{2,1,0:T(2,128)(2,1)S(1)} %bitcast.146), channel_id=1, replica_groups=mesh['dev'=32] {'dev'}, dimensions={0}, use_global_device_ids=true | all-gather | bytes 8448 | tf_op jit(solution)/shard_map/all_gather | solution.py:67
  276.6 28.6 %collective-permute-done.5 = bf16[384,2048]{1,0:T(8,128)(2,1)S(1)} collective-permute-done((bf16[384,2048]{1,0:T(8,128)(2,1)}, bf16[384,2048]{1,0:T(8,128)(2,1)S(1)}, u32[]{:S(2)}, u32[]{:S(2)}) %collective-permute-start.5) | collective-permute-done | bytes 1572896 | tf_op jit(solution)/shard_map/ppermute | solution.py:16
  305.3 16.1 collective-permute-done.6
  325.1 5.6 fusion.104
  330.7 9.8 copy.60
  340.5 13.8 copy.63
  354.3 9.8 copy.61
  364.1 13.7 copy.64
  378.0 152.7 %while.28 = (s32[]{:T(128)}, bf16[16,384,64]{1,2,0:T(8,128)(2,1)S(1)}, f32[16,384]{1,0:T(8,128)S(1)}, bf16[16,384,64]{2,1,0:T(8,128)(2,1)}, bf16[16,3456,64]{2,1...) while((s32[]{:T(128)}, ...), condition=%wide.region_8.9_spmd.clone, body=%wide.region_5.8_spmd.clone.sunk | while | flops 351682176 | bytes 39161988 | solution.py:135
  383.6 4.0 fusion.143
  393.1 4.0 fusion.143
  402.6 4.0 fusion.143
  412.2 4.0 fusion.143
  421.7 4.0 fusion.143
  431.3 4.0 fusion.143
  440.9 4.0 fusion.143
  450.5 4.0 fusion.143
  469.5 4.0 fusion.143
  479.0 4.0 fusion.143
  498.1 4.0 fusion.143
  507.6 4.0 fusion.143
  526.6 4.0 fusion.143
  534.8 20.7 %multiply_convert_fusion.1 = (bf16[384,4096]{1,0:T(8,128)(2,1)}, f32[384,4096]{1,0:T(8,128)}, f32[384,4096]{1,0:T(8,128)}) fusion(f32[4096]{0:T(1024)S(1)} %bitcast.143, bf16[1024,4096]{1,0:T(8,128)(2,1)} %all-gather.10.cloned.1.call-done, f32[384,1024]{1,0:T(8,128)S(1)} %get-tuple-element.290, f32[1024]{0:T(1024)S(1)} %convert_element_type.168, ...), kind=kOutput, calls=%fused_computation.63 | convolution fusion | flops 3327000576 | bytes 25717760 | tf_op jit(solution)/shard_map/dot_general | solution.py:143
  555.6 13.8 fusion.106
  569.3 4.3 multiply_reduce_fusion.1
  573.7 8.3 fusion.74
  589.2 192.4 %while.29 = (s32[]{:T(128)}, bf16[16,384,64]{1,2,0:T(8,128)(2,1)S(1)}, f32[16,3456,64]{1,2,0:T(8,128)}, f32[16,3456,64]{1,2,0:T(8,128)}, bf16[16,384,64]{2,1,0:T...) while((s32[]{:T(128)}, ...), condition=%wide.region_15.16_spmd.clone, body=%wide.region_13.15_spmd.clone.sunk | while | flops 862862976 | bytes 44658296 | solution.py:223
  781.6 13.3 fusion.47
  794.9 4.8 fusion.103
  805.4 48.1 %collective-permute-start.13 = (bf16[384,2048]{0,1:T(8,128)(2,1)}, bf16[384,2048]{0,1:T(8,128)(2,1)S(1)}, u32[]{:S(2)}, u32[]{:S(2)}) collective-permute-start(bf16[384,2048]{0,1:T(8,128)(2,1)} %get-tuple-element.298), channel_id=1, source_target_pairs={{0,2},{1,3},{2,4},{3,5},{4,6},{5,7},{6,8},{7,9},{8,10},{9,11},{10,... | collective-permute-start | bytes 4718600 | tf_op jit(solution)/shard_map/ppermute | solution.py:16
  853.5 45.7 %collective-permute-start.14 = (bf16[384,2048]{0,1:T(8,128)(2,1)}, bf16[384,2048]{0,1:T(8,128)(2,1)S(1)}, u32[]{:S(2)}, u32[]{:S(2)}) collective-permute-start(bf16[384,2048]{0,1:T(8,128)(2,1)} %get-tuple-element.297), channel_id=1, source_target_pairs={{0,3},{1,4},{2,5},{3,6},{4,7},{5,8},{6,9},{7,10},{8,11},{9,12},{10... | collective-permute-start | bytes 4718600 | tf_op jit(solution)/shard_map/ppermute | solution.py:16
  899.2 27.8 %collective-permute-start.15 = (bf16[384,2048]{0,1:T(8,128)(2,1)}, bf16[384,2048]{0,1:T(8,128)(2,1)S(1)}, u32[]{:S(2)}, u32[]{:S(2)}) collective-permute-start(bf16[384,2048]{0,1:T(8,128)(2,1)} %get-tuple-element.296), channel_id=1, source_target_pairs={{0,4},{1,5},{2,6},{3,7},{4,8},{5,9},{6,10},{7,11},{8,12},{9,13},{1... | collective-permute-start | bytes 4718600 | tf_op jit(solution)/shard_map/ppermute | solution.py:16
  931.2 39.8 %collective-permute-done.14 = bf16[384,2048]{0,1:T(8,128)(2,1)S(1)} collective-permute-done((bf16[384,2048]{0,1:T(8,128)(2,1)}, bf16[384,2048]{0,1:T(8,128)(2,1)S(1)}, u32[]{:S(2)}, u32[]{:S(2)}) %collective-permute-start.14) | collective-permute-done | bytes 1572896 | tf_op jit(solution)/shard_map/ppermute | solution.py:16
  972.2 73.6 %collective-permute-done.15 = bf16[384,2048]{0,1:T(8,128)(2,1)S(1)} collective-permute-done((bf16[384,2048]{0,1:T(8,128)(2,1)}, bf16[384,2048]{0,1:T(8,128)(2,1)S(1)}, u32[]{:S(2)}, u32[]{:S(2)}) %collective-permute-start.15) | collective-permute-done | bytes 1572896 | tf_op jit(solution)/shard_map/ppermute | solution.py:16
  1048.3 7.3 fusion.60
  1055.7 8.1 fusion.81
  1064.1 12.8 fusion.77
  1078.0 10.1 fusion.83
  1089.8 6.2 fusion.98
  1098.0 104.9 %all-reduce.19 = (f32[1024]{0:T(1024)S(1)}, f32[1024]{0:T(1024)S(1)}, f32[2048]{0:T(1024)S(1)}, f32[1024]{0:T(1024)S(1)}, f32[1024]{0:T(1024)S(1)}, /*index=5*/f...) all-reduce(f32[1024]{0:T(1024)S(1)} %get-tuple-element.218, ...), channel_id=2, replica_groups=mesh['dev'=32] {'dev'}, use_global_device_ids=true, to_apply=%region_19.20.clone | all-reduce | flops 14336 | bytes 114688
  1212.2 70.6 %reduce-scatter.5.cloned.1.call-done = f32[32,3072]{1,0:T(8,128)} async-done(((f32[1024,3072]{1,0:T(8,128)}), f32[32,3072]{1,0:T(8,128)}) %reduce-scatter.5.cloned.1.call-update) | async-done | bytes 393232 | tf_op jit(solution)/shard_map/reduce_scatter | solution.py:253
  1282.7 185.0 %reduce-scatter.9.cloned.1.call-done = f32[32,4096]{1,0:T(8,128)} async-done(((f32[1024,4096]{1,0:T(8,128)}), f32[32,4096]{1,0:T(8,128)}) %reduce-scatter.9.cloned.1.call-update) | async-done | bytes 524304 | tf_op jit(solution)/shard_map/reduce_scatter | solution.py:260
  1467.7 187.5 %reduce-scatter.11.cloned.1.call-done = f32[128,1024]{1,0:T(8,128)} async-done(((f32[4096,1024]{1,0:T(8,128)}), f32[128,1024]{1,0:T(8,128)}) %reduce-scatter.11.cloned.1.call-update) | async-done | bytes 524304 | tf_op jit(solution)/shard_map/reduce_scatter | solution.py:262
  (435 shorter events, 372.4 us)
Async XLA Ops:
  7.2 76.1 %all-gather.6.cloned.1.call-start = ((), (), s32[]{:S(2)}) async-start(), calls=%async_computation.4 | async-start | bytes 6488064 | tf_op jit(solution)/shard_map/all_gather | solution.py:59
  7.9 522.7 %all-gather.8.cloned.1.call-start = ((), (), s32[]{:S(2)}) async-start(), calls=%async_computation.5 | async-start | bytes 2162688 | tf_op jit(solution)/shard_map/all_gather | solution.py:61
  8.7 526.1 %all-gather.10.cloned.1.call-start = ((), (), s32[]{:S(2)}) async-start(), calls=%async_computation.6 | async-start | bytes 8650752 | tf_op jit(solution)/shard_map/all_gather | solution.py:66
  9.4 546.2 %all-gather.12.cloned.1.call-start = ((), (), s32[]{:S(2)}) async-start(), calls=%async_computation.7 | async-start | bytes 8650752 | tf_op jit(solution)/shard_map/all_gather | solution.py:68
  59.6 28.8 %copy-start.19 = (f32[1024]{0:T(1024)}, f32[1024]{0:T(1024)S(1)}, u32[]{:S(2)}) copy-start(f32[1024]{0:T(1024)S(1)} %convert_element_type.154) | copy-start | bytes 12292
  59.6 28.9 %copy-start.21 = (f32[1024]{0:T(1024)}, f32[1024]{0:T(1024)S(1)}, u32[]{:S(2)}) copy-start(f32[1024]{0:T(1024)S(1)} %convert_element_type.155) | copy-start | bytes 12292
  60.9 27.5 %copy-start.23 = (f32[384]{0:T(512)}, f32[384]{0:T(512)S(1)}, u32[]{:S(2)}) copy-start(f32[384]{0:T(512)S(1)} %broadcast_multiply_fusion.1) | copy-start | bytes 4612
  63.0 25.5 %copy-start.25 = (f32[384]{0:T(512)}, f32[384]{0:T(512)S(1)}, u32[]{:S(2)}) copy-start(f32[384]{0:T(512)S(1)} %fusion.90) | copy-start | bytes 4612
  88.6 13.9 copy-start.35
  88.6 18.2 %copy-start.33 = (bf16[128]{0:T(256)(128)(2,1)S(1)}, bf16[128]{0:T(256)(128)(2,1)}, u32[]{:S(2)}) copy-start(bf16[128]{0:T(256)(128)(2,1)} %param.34) | copy-start | bytes 772
  90.3 173.6 %collective-permute-start = (bf16[384,2048]{1,0:T(8,128)(2,1)}, bf16[384,2048]{1,0:T(8,128)(2,1)}, u32[]{:S(2)}, u32[]{:S(2)}) collective-permute-start(bf16[384,2048]{1,0:T(8,128)(2,1)} %pad_maximum_fusion.2), channel_id=1, source_target_pairs={{0,4},{1,5},{2,6},{3,7},{4,8},{5,9},{6,10},{7,11},{8,12},{9,13},{1... | collective-permute-start | bytes 4718600 | tf_op jit(solution)/shard_map/ppermute | solution.py:16
  94.9 172.1 %collective-permute-start.1 = (bf16[384,2048]{1,0:T(8,128)(2,1)}, bf16[384,2048]{1,0:T(8,128)(2,1)}, u32[]{:S(2)}, u32[]{:S(2)}) collective-permute-start(bf16[384,2048]{1,0:T(8,128)(2,1)} %pad_maximum_fusion.2), channel_id=1, source_target_pairs={{0,3},{1,4},{2,5},{3,6},{4,7},{5,8},{6,9},{7,10},{8,11},{9,12},{10... | collective-permute-start | bytes 4718600 | tf_op jit(solution)/shard_map/ppermute | solution.py:16
  98.2 171.7 %collective-permute-start.2 = (bf16[384,2048]{1,0:T(8,128)(2,1)}, bf16[384,2048]{1,0:T(8,128)(2,1)}, u32[]{:S(2)}, u32[]{:S(2)}) collective-permute-start(bf16[384,2048]{1,0:T(8,128)(2,1)} %pad_maximum_fusion.2), channel_id=1, source_target_pairs={{0,2},{1,3},{2,4},{3,5},{4,6},{5,7},{6,8},{7,9},{8,10},{9,11},{10,... | collective-permute-start | bytes 4718600 | tf_op jit(solution)/shard_map/ppermute | solution.py:16
  102.5 1109.7 %reduce-scatter.7.cloned.1.call-start = ((), (), s32[]{:S(2)}) async-start(), calls=%async_computation.9 | async-start | bytes 4325376 | tf_op jit(solution)/shard_map/reduce_scatter | solution.py:255
  102.7 170.5 %collective-permute-start.3 = (bf16[384,2048]{1,0:T(8,128)(2,1)}, bf16[384,2048]{1,0:T(8,128)(2,1)}, u32[]{:S(2)}, u32[]{:S(2)}) collective-permute-start(bf16[384,2048]{1,0:T(8,128)(2,1)} %pad_maximum_fusion.2), channel_id=1, source_target_pairs={{0,1},{1,2},{2,3},{3,4},{4,5},{5,6},{6,7},{7,8},{8,9},{9,10},{10,1... | collective-permute-start | bytes 4718600 | tf_op jit(solution)/shard_map/ppermute | solution.py:16
  105.3 169.6 %collective-permute-start.4 = (bf16[384,2048]{1,0:T(8,128)(2,1)}, bf16[384,2048]{1,0:T(8,128)(2,1)}, u32[]{:S(2)}, u32[]{:S(2)}) collective-permute-start(bf16[384,2048]{1,0:T(8,128)(2,1)} %pad_maximum_fusion.2), channel_id=1, source_target_pairs={{1,0},{2,1},{3,2},{4,3},{5,4},{6,5},{7,6},{8,7},{9,8},{10,9},{11,1... | collective-permute-start | bytes 4718600 | tf_op jit(solution)/shard_map/ppermute | solution.py:16
  264.0 41.2 %collective-permute-start.5 = (bf16[384,2048]{1,0:T(8,128)(2,1)}, bf16[384,2048]{1,0:T(8,128)(2,1)S(1)}, u32[]{:S(2)}, u32[]{:S(2)}) collective-permute-start(bf16[384,2048]{1,0:T(8,128)(2,1)} %pad_maximum_fusion.2), channel_id=1, source_target_pairs={{2,0},{3,1},{4,2},{5,3},{6,4},{7,5},{8,6},{9,7},{10,8},{11,9},{12,... | collective-permute-start | bytes 4718600 | tf_op jit(solution)/shard_map/ppermute | solution.py:16
  267.0 54.4 %collective-permute-start.6 = (bf16[384,2048]{1,0:T(8,128)(2,1)}, bf16[384,2048]{1,0:T(8,128)(2,1)S(1)}, u32[]{:S(2)}, u32[]{:S(2)}) collective-permute-start(bf16[384,2048]{1,0:T(8,128)(2,1)} %pad_maximum_fusion.2), channel_id=1, source_target_pairs={{3,0},{4,1},{5,2},{6,3},{7,4},{8,5},{9,6},{10,7},{11,8},{12,9},{13... | collective-permute-start | bytes 4718600 | tf_op jit(solution)/shard_map/ppermute | solution.py:16
  269.9 55.1 %collective-permute-start.7 = (bf16[384,2048]{1,0:T(8,128)(2,1)}, bf16[384,2048]{1,0:T(8,128)(2,1)S(1)}, u32[]{:S(2)}, u32[]{:S(2)}) collective-permute-start(bf16[384,2048]{1,0:T(8,128)(2,1)} %pad_maximum_fusion.2), channel_id=1, source_target_pairs={{4,0},{5,1},{6,2},{7,3},{8,4},{9,5},{10,6},{11,7},{12,8},{13,9},{1... | collective-permute-start | bytes 4718600 | tf_op jit(solution)/shard_map/ppermute | solution.py:16
  378.0 152.7 %copy-start.1 = (bf16[384,1024]{1,0:T(8,128)(2,1)S(1)}, bf16[384,1024]{1,0:T(8,128)(2,1)}, u32[]{:S(2)}) copy-start(bf16[384,1024]{1,0:T(8,128)(2,1)} %param.21) | copy-start | bytes 2359300
  534.5 39.2 %copy-start.4 = (f32[384,1024]{1,0:T(8,128)}, f32[384,1024]{1,0:T(8,128)S(1)}, u32[]{:S(2)}) copy-start(f32[384,1024]{1,0:T(8,128)S(1)} %get-tuple-element.290) | copy-start | bytes 4718596
  534.8 20.8 %copy-start.9 = (bf16[384,1024]{1,0:T(8,128)(2,1)S(1)}, bf16[384,1024]{1,0:T(8,128)(2,1)}, u32[]{:S(2)}) copy-start(bf16[384,1024]{1,0:T(8,128)(2,1)} %param.22) | copy-start | bytes 2359300
  555.6 13.8 copy-start.34
  573.7 8.4 copy-start.6
  573.7 8.4 copy-start.10
  585.8 696.9 %reduce-scatter.5.cloned.1.call-start = ((), (), s32[]{:S(2)}) async-start(), calls=%async_computation.8 | async-start | bytes 12976128 | tf_op jit(solution)/shard_map/reduce_scatter | solution.py:253
  781.5 266.7 %slice-start = ((s8[14155776]{0:T(1024)(128)(4,1)}), s8[4194304]{0:T(1024)(128)(4,1)S(1)}, s32[]{:S(2)}) async-start(s8[14155776]{0:T(1024)(128)(4,1)} %bitcast.130), calls=%async_computation.12 | async-start | bytes 8388608
  781.6 266.7 %slice-start.1 = ((s8[14155776]{0:T(1024)(128)(4,1)}), s8[4194304]{0:T(1024)(128)(4,1)S(1)}, s32[]{:S(2)}) async-start(s8[14155776]{0:T(1024)(128)(4,1)} %bitcast.130), calls=%async_computation.13 | async-start | bytes 8388608
  781.6 266.7 %slice-start.2 = ((s8[14155776]{0:T(1024)(128)(4,1)}), s8[4194304]{0:T(1024)(128)(4,1)S(1)}, s32[]{:S(2)}) async-start(s8[14155776]{0:T(1024)(128)(4,1)} %bitcast.130), calls=%async_computation.14 | async-start | bytes 8388608
  794.8 253.4 %slice-start.3 = ((s8[14155776]{0:T(1024)(128)(4,1)}), s8[1572864]{0:T(1024)(128)(4,1)S(1)}, s32[]{:S(2)}) async-start(s8[14155776]{0:T(1024)(128)(4,1)} %bitcast.130), calls=%async_computation.15 | async-start | bytes 3145728
  799.7 99.6 %collective-permute-start.10 = (bf16[384,2048]{0,1:T(8,128)(2,1)}, bf16[384,2048]{0,1:T(8,128)(2,1)S(1)}, u32[]{:S(2)}, u32[]{:S(2)}) collective-permute-start(bf16[384,2048]{0,1:T(8,128)(2,1)} %get-tuple-element.301), channel_id=1, source_target_pairs={{2,0},{3,1},{4,2},{5,3},{6,4},{7,5},{8,6},{9,7},{10,8},{11,9},{12,... | collective-permute-start | bytes 4718600 | tf_op jit(solution)/shard_map/ppermute | solution.py:16
  801.0 126.1 %collective-permute-start.11 = (bf16[384,2048]{0,1:T(8,128)(2,1)}, bf16[384,2048]{0,1:T(8,128)(2,1)S(1)}, u32[]{:S(2)}, u32[]{:S(2)}) collective-permute-start(bf16[384,2048]{0,1:T(8,128)(2,1)} %get-tuple-element.300), channel_id=1, source_target_pairs={{1,0},{2,1},{3,2},{4,3},{5,4},{6,5},{7,6},{8,7},{9,8},{10,9},{11,1... | collective-permute-start | bytes 4718600 | tf_op jit(solution)/shard_map/ppermute | solution.py:16
  802.3 126.1 %collective-permute-start.12 = (bf16[384,2048]{0,1:T(8,128)(2,1)}, bf16[384,2048]{0,1:T(8,128)(2,1)S(1)}, u32[]{:S(2)}, u32[]{:S(2)}) collective-permute-start(bf16[384,2048]{0,1:T(8,128)(2,1)} %get-tuple-element.299), channel_id=1, source_target_pairs={{0,1},{1,2},{2,3},{3,4},{4,5},{5,6},{6,7},{7,8},{8,9},{9,10},{10,1... | collective-permute-start | bytes 4718600 | tf_op jit(solution)/shard_map/ppermute | solution.py:16
  805.4 124.7 %collective-permute-start.13 = (bf16[384,2048]{0,1:T(8,128)(2,1)}, bf16[384,2048]{0,1:T(8,128)(2,1)S(1)}, u32[]{:S(2)}, u32[]{:S(2)}) collective-permute-start(bf16[384,2048]{0,1:T(8,128)(2,1)} %get-tuple-element.298), channel_id=1, source_target_pairs={{0,2},{1,3},{2,4},{3,5},{4,6},{5,7},{6,8},{7,9},{8,10},{9,11},{10,... | collective-permute-start | bytes 4718600 | tf_op jit(solution)/shard_map/ppermute | solution.py:16
  853.5 117.5 %collective-permute-start.14 = (bf16[384,2048]{0,1:T(8,128)(2,1)}, bf16[384,2048]{0,1:T(8,128)(2,1)S(1)}, u32[]{:S(2)}, u32[]{:S(2)}) collective-permute-start(bf16[384,2048]{0,1:T(8,128)(2,1)} %get-tuple-element.297), channel_id=1, source_target_pairs={{0,3},{1,4},{2,5},{3,6},{4,7},{5,8},{6,9},{7,10},{8,11},{9,12},{10... | collective-permute-start | bytes 4718600 | tf_op jit(solution)/shard_map/ppermute | solution.py:16
  899.2 29.2 %copy-start.12 = (bf16[384,2048]{0,1:T(8,128)(2,1)}, bf16[384,2048]{0,1:T(8,128)(2,1)S(1)}, u32[]{:S(2)}) copy-start(bf16[384,2048]{0,1:T(8,128)(2,1)S(1)} %collective-permute-done.10) | copy-start | bytes 4718596
  899.2 146.6 %collective-permute-start.15 = (bf16[384,2048]{0,1:T(8,128)(2,1)}, bf16[384,2048]{0,1:T(8,128)(2,1)S(1)}, u32[]{:S(2)}, u32[]{:S(2)}) collective-permute-start(bf16[384,2048]{0,1:T(8,128)(2,1)} %get-tuple-element.296), channel_id=1, source_target_pairs={{0,4},{1,5},{2,6},{3,7},{4,8},{5,9},{6,10},{7,11},{8,12},{9,13},{1... | collective-permute-start | bytes 4718600 | tf_op jit(solution)/shard_map/ppermute | solution.py:16
  927.1 120.0 %collective-permute-start.8 = (bf16[384,2048]{0,1:T(8,128)(2,1)}, bf16[384,2048]{0,1:T(8,128)(2,1)S(1)}, u32[]{:S(2)}, u32[]{:S(2)}) collective-permute-start(bf16[384,2048]{0,1:T(8,128)(2,1)} %get-tuple-element.295), channel_id=1, source_target_pairs={{4,0},{5,1},{6,2},{7,3},{8,4},{9,5},{10,6},{11,7},{12,8},{13,9},{1... | collective-permute-start | bytes 4718600 | tf_op jit(solution)/shard_map/ppermute | solution.py:16
  928.4 127.2 %copy-start.2 = (bf16[384,1024]{1,0:T(8,128)(2,1)S(1)}, bf16[384,1024]{1,0:T(8,128)(2,1)}, u32[]{:S(2)}) copy-start(bf16[384,1024]{1,0:T(8,128)(2,1)} %param.21) | copy-start | bytes 2359300
  928.4 127.2 %copy-start.20 = (f32[1024]{0:T(1024)S(1)}, f32[1024]{0:T(1024)}, u32[]{:S(2)}) copy-start(f32[1024]{0:T(1024)} %copy-done.19) | copy-start | bytes 12292
  928.4 127.2 %copy-start.22 = (f32[1024]{0:T(1024)S(1)}, f32[1024]{0:T(1024)}, u32[]{:S(2)}) copy-start(f32[1024]{0:T(1024)} %copy-done.21) | copy-start | bytes 12292
  928.5 127.2 %copy-start.24 = (f32[384]{0:T(512)S(1)}, f32[384]{0:T(512)}, u32[]{:S(2)}) copy-start(f32[384]{0:T(512)} %copy-done.23) | copy-start | bytes 4612
  928.5 127.2 %copy-start.26 = (f32[384]{0:T(512)S(1)}, f32[384]{0:T(512)}, u32[]{:S(2)}) copy-start(f32[384]{0:T(512)} %copy-done.25) | copy-start | bytes 4612
  928.5 119.8 %collective-permute-start.9 = (bf16[384,2048]{0,1:T(8,128)(2,1)}, bf16[384,2048]{0,1:T(8,128)(2,1)}, u32[]{:S(2)}, u32[]{:S(2)}) collective-permute-start(bf16[384,2048]{0,1:T(8,128)(2,1)} %get-tuple-element.302), channel_id=1, source_target_pairs={{3,0},{4,1},{5,2},{6,3},{7,4},{8,5},{9,6},{10,7},{11,8},{12,9},{13... | collective-permute-start | bytes 4718600 | tf_op jit(solution)/shard_map/ppermute | solution.py:16
  1063.8 403.9 %reduce-scatter.9.cloned.1.call-start = ((), (), s32[]{:S(2)}) async-start(), calls=%async_computation.10 | async-start | bytes 17301504 | tf_op jit(solution)/shard_map/reduce_scatter | solution.py:260
  1076.9 578.3 %reduce-scatter.11.cloned.1.call-start = ((), (), s32[]{:S(2)}) async-start(), calls=%async_computation.11 | async-start | bytes 17301504 | tf_op jit(solution)/shard_map/reduce_scatter | solution.py:262
  1089.8 8.2 copy-start.29
  1089.8 8.2 copy-start.30
  (31 other events, 78.7 us)
Sparse Core Ops, SparseCore 0:
  10.9 72.4 all-gather.5
  86.2 109.7 all-gather.7
  198.8 82.1 all-gather.9
  283.8 157.3 all-gather.11
  585.9 223.8 reduce-scatter.6
  1063.9 218.7 reduce-scatter.4
  1285.7 182.0 reduce-scatter.8
  1470.7 184.4 reduce-scatter.10
where the time goes:
time: 1670 us; the launch traced here: 1660 us
  waiting for transfers between devices  627 us (38%)
  matrix products  378 us (23%)
  blocking collectives  302 us (18%)
  starting transfers between devices  151 us (9%)
  local copies, waits for them, and re-layouts  128 us (8%)
  other arithmetic  59.5 us (4%)
    reduce_scatter x1, waiting for transfers between devices, body(): lax.psum_scatter(d_fc2, 'dev', scatter_dimension=0, tiled=True)  187 us
    reduce_scatter x1, waiting for transfers between devices, body(): lax.psum_scatter(d_fc1, 'dev', scatter_dimension=0, tiled=True)  185 us
    ppermute x16, waiting for transfers between devices, shifted(): return lax.ppermute(shard, axis, pairs)  162 us
    all_gather x1, blocking collectives, body(): lax.all_gather(fc1_bias, 'dev', axis=0, tiled=True)  155 us
    ppermute x16, starting transfers between devices, shifted(): return lax.ppermute(shard, axis, pairs)  150 us
    unnamed x2, blocking collectives  147 us
    reduce_scatter x1, waiting for transfers between devices, body(): lax.psum_scatter(d_qkv_weight, 'dev', scatter_dimension=0, tiled=True)  70.6 us
    dot_general x16, matrix products, head_forward(): out = jnp.dot(prob, v_one, preferred_element_type=jnp.float32)  63.6 us
  transfers between devices with their start and end apart: 24, of which 9 were waited for; matrix products, arithmetic and copies ran while one was open for 30% of the time, Pallas kernels for 0%

commit v1 on v0

v1 whole, which is shorter than its diff:
```python
import jax
import jax.numpy as jnp
from jax import lax
from jax.sharding import PartitionSpec as P
from jax.experimental import pallas as pl
from jax.experimental.pallas import tpu as pltpu

BQ = 256
BK = 256
HD = 64
LOG2E = 1.4426950408889634
SCALE = 0.125
MASKED = -1e30
NT = (((1,), (1,)), ((), ()))


def rows_of(ref, block, size):
    return ref[pl.ds(pl.multiple_of(block * size, size), size), :]


def head_halves(block):
    first = lax.broadcasted_iota(jnp.int32, block.shape, 1) < HD
    zero = jnp.zeros_like(block)
    return jnp.where(first, block, zero), jnp.where(first, zero, block)


def transpose_into(target, source):
    for j in range(source.shape[0] // BK):
        part = source[j * BK : (j + 1) * BK, :].astype(jnp.float32)
        target[:, j * BK : (j + 1) * BK] = part.T.astype(target.dtype)


def forward_kernel(low, high, seg, q_ref, k_ref, v_ref, o_ref, lse_ref, v_t):
    step = pl.program_id(0)

    @pl.when(step == 0)
    def _():
        transpose_into(v_t, v_ref)

    q_heads = head_halves(q_ref[...])
    begin, end = seg[0:1, :], seg[1:2, :]
    place = lax.broadcasted_iota(jnp.int32, (BK, BQ), 0)

    def one_block(j, carry):
        keys = rows_of(k_ref, j, BK)
        at = place + j * BK
        valid = (at >= begin) & (at < end)
        out = []
        for h in range(2):
            top, total, acc = carry[h]
            s = lax.dot_general(keys, q_heads[h], NT, preferred_element_type=jnp.float32)
            s = jnp.where(valid, s * (SCALE * LOG2E), MASKED)
            new_top = jnp.maximum(top, jnp.max(s, axis=0, keepdims=True))
            p = jnp.exp2(s - new_top)
            fade = jnp.exp2(top - new_top)
            total = total * fade + jnp.sum(p, axis=0, keepdims=True)
            v_part = v_t[h * HD : (h + 1) * HD, pl.ds(pl.multiple_of(j * BK, BK), BK)]
            acc = acc * fade + jnp.dot(v_part, p.astype(jnp.bfloat16), preferred_element_type=jnp.float32)
            out.append((new_top, total, acc))
        return tuple(out)

    start = (
        jnp.full((1, BQ), MASKED, jnp.float32),
        jnp.zeros((1, BQ), jnp.float32),
        jnp.zeros((HD, BQ), jnp.float32),
    )
    done = lax.fori_loop(low[step], high[step], one_block, (start, start))
    outs = jnp.concatenate([acc / total for _, total, acc in done], axis=0)
    o_ref[...] = outs.T.astype(o_ref.dtype)
    for h in range(2):
        top, total, _ = done[h]
        lse_ref[h : h + 1, :] = top + jnp.log2(total)


def backward_kernel(
    low, high, seg, q_ref, k_ref, v_ref, o_ref, do_ref, lse_ref, dq_ref, mid_ref, edge_ref, k_t, dk, dv, dq_t
):
    step = pl.program_id(0)

    @pl.when(step == 0)
    def _():
        transpose_into(k_t, k_ref)
        dk[...] = jnp.zeros_like(dk)
        dv[...] = jnp.zeros_like(dv)

    q_heads = head_halves(q_ref[...])
    do_heads = head_halves(do_ref[...])
    q_both = jnp.concatenate(q_heads, axis=0)
    do_both = jnp.concatenate(do_heads, axis=0)
    prod = (do_ref[...].astype(jnp.float32) * o_ref[...].astype(jnp.float32)).T
    begin, end = seg[0:1, :], seg[1:2, :]
    place = lax.broadcasted_iota(jnp.int32, (BK, BQ), 0)
    centre = [jnp.sum(prod[h * HD : (h + 1) * HD], axis=0, keepdims=True) for h in range(2)]
    lse = [lse_ref[h : h + 1, :] for h in range(2)]
    dq_t[...] = jnp.zeros_like(dq_t)

    @pl.loop(low[step], high[step])
    def _(j):
        rows = pl.ds(pl.multiple_of(j * BK, BK), BK)
        keys, values = k_ref[rows, :], v_ref[rows, :]
        at = place + j * BK
        valid = (at >= begin) & (at < end)
        ps, dss = [], []
        for h in range(2):
            s = lax.dot_general(keys, q_heads[h], NT, preferred_element_type=jnp.float32)
            p = jnp.where(valid, jnp.exp2(s * (SCALE * LOG2E) - lse[h]), 0.0)
            dp = lax.dot_general(values, do_heads[h], NT, preferred_element_type=jnp.float32)
            ds = (p * (dp - centre[h])).astype(jnp.bfloat16)
            ps.append(p.astype(jnp.bfloat16))
            dss.append(ds)
            part = slice(h * HD, (h + 1) * HD)
            dq_t[part, :] += jnp.dot(k_t[part, rows], ds, preferred_element_type=jnp.float32)
        dv[rows, :] += jnp.dot(jnp.concatenate(ps, axis=1), do_both, preferred_element_type=jnp.float32)
        dk[rows, :] += jnp.dot(jnp.concatenate(dss, axis=1), q_both, preferred_element_type=jnp.float32)

    dq_ref[...] = (dq_t[...] * SCALE).T.astype(dq_ref.dtype)

    @pl.when(step == pl.num_programs(0) - 1)
    def _():
        halo = edge_ref.shape[1]
        span = mid_ref.shape[0]
        for j in range(dk.shape[0] // BK):
            part = slice(j * BK, (j + 1) * BK)
            both = jnp.concatenate([dk[part] * SCALE, dv[part]], axis=1)
            if j * BK < halo:
                edge_ref[0, part, :] = both.astype(edge_ref.dtype)
            elif j * BK < halo + span:
                mid_ref[j * BK - halo : (j + 1) * BK - halo, :] = both
            else:
                first = j * BK - halo - span
                edge_ref[1, first : first + BK, :] = both.astype(edge_ref.dtype)


def attention_forward(low, high, seg, q, k, v):
    span, width = q.shape
    window = k.shape[0]
    steps = span // BQ
    whole = pl.BlockSpec((window, width), lambda i, *_: (0, 0))
    rows = pl.BlockSpec((BQ, width), lambda i, *_: (i, 0))
    return pl.pallas_call(
        forward_kernel,
        out_shape=(
            jax.ShapeDtypeStruct((span, width), jnp.bfloat16),
            jax.ShapeDtypeStruct((8, span), jnp.float32),
        ),
        grid_spec=pltpu.PrefetchScalarGridSpec(
            num_scalar_prefetch=2,
            grid=(steps,),
            in_specs=[pl.BlockSpec((2, BQ), lambda i, *_: (0, i)), rows, whole, whole],
            out_specs=[rows, pl.BlockSpec((8, BQ), lambda i, *_: (0, i))],
            scratch_shapes=[pltpu.VMEM((width, window), jnp.bfloat16)],
        ),
        compiler_params=pltpu.CompilerParams(vmem_limit_bytes=40 << 20),
        cost_estimate=pl.CostEstimate(flops=16 * span * 1536 * 128, bytes_accessed=8 << 20, transcendentals=2 * span * 1536),
        name="attention_forward",
    )(low, high, seg, q, k, v)


def attention_backward(low, high, seg, q, k, v, o, do, lse, halo):
    span, width = q.shape
    window = k.shape[0]
    steps = span // BQ
    whole = pl.BlockSpec((window, width), lambda i, *_: (0, 0))
    rows = pl.BlockSpec((BQ, width), lambda i, *_: (i, 0))
    return pl.pallas_call(
        backward_kernel,
        out_shape=(
            jax.ShapeDtypeStruct((span, width), jnp.bfloat16),
            jax.ShapeDtypeStruct((span, 2 * width), jnp.float32),
            jax.ShapeDtypeStruct((2, halo, 2 * width), jnp.bfloat16),
        ),
        grid_spec=pltpu.PrefetchScalarGridSpec(
            num_scalar_prefetch=2,
            grid=(steps,),
            in_specs=[
                pl.BlockSpec((2, BQ), lambda i, *_: (0, i)), rows, whole, whole, rows, rows,
                pl.BlockSpec((8, BQ), lambda i, *_: (0, i)),
            ],
            out_specs=[
                rows,
                pl.BlockSpec((span, 2 * width), lambda i, *_: (0, 0)),
                pl.BlockSpec((2, halo, 2 * width), lambda i, *_: (0, 0, 0)),
            ],
            scratch_shapes=[
                pltpu.VMEM((width, window), jnp.bfloat16),
                pltpu.VMEM((window, width), jnp.float32),
                pltpu.VMEM((window, width), jnp.float32),
                pltpu.VMEM((width, BQ), jnp.float32),
            ],
        ),
        compiler_params=pltpu.CompilerParams(vmem_limit_bytes=48 << 20),
        cost_estimate=pl.CostEstimate(flops=40 * span * 1536 * 128, bytes_accessed=16 << 20, transcendentals=2 * span * 1536),
        name="attention_backward",
    )(low, high, seg, q, k, v, o, do, lse)


HEADS = 16
SEQ = 1370
GROUP = 8
EPS = 1e-06
F32, BF16 = jnp.float32, jnp.bfloat16


def mm(left, right):
    return jnp.dot(left, right, preferred_element_type=F32)


def mm_t(left, right):
    return jnp.einsum("tf,df->td", left, right, preferred_element_type=F32)


def t_mm(left, right):
    return jnp.einsum("td,tf->df", left, right, preferred_element_type=F32)


def normalised(value):
    centre = value - jnp.mean(value, axis=-1, keepdims=True)
    rstd = lax.rsqrt(jnp.mean(centre * centre, axis=-1, keepdims=True) + EPS)
    return centre * rstd, rstd


def norm_back(unit, rstd, grad):
    first = jnp.mean(grad, axis=-1, keepdims=True)
    second = jnp.mean(grad * unit, axis=-1, keepdims=True)
    return rstd * (grad - first - unit * second)


def gelu_parts(z):
    half = 0.5 * (1.0 + lax.erf(z * 0.7071067811865476))
    slope = half + z * (0.3989422804014327 * jnp.exp(-0.5 * z * z))
    return z * half, slope


def groups_of(count):
    return [list(range(first, first + GROUP)) for first in range(0, count, GROUP)]


def gathered(shard):
    return lax.all_gather(shard, "dev", axis=0, tiled=True)


def scattered(whole):
    return lax.psum_scatter(whole, "dev", scatter_dimension=0, tiled=True)


def pack(vectors, count):
    return jnp.concatenate([v.reshape(count, -1) for v in vectors], axis=1)


def unpack(packed, sizes):
    out, at = [], 0
    for size in sizes:
        out.append(packed[:, at : at + size].reshape(-1))
        at += size
    return out


def to_heads(parts, devices):
    rows = parts[0].shape[0]
    sent = jnp.stack([p.reshape(rows, GROUP, -1) for p in parts], axis=2)
    sent = sent.transpose(1, 0, 2, 3)
    back = lax.all_to_all(sent, "dev", 0, 0, axis_index_groups=groups_of(devices), tiled=True)
    return [back[:, :, i].reshape(GROUP * rows, -1) for i in range(len(parts))]


def to_tokens(parts, devices):
    rows = parts[0].shape[0] // GROUP
    sent = jnp.stack([p.reshape(GROUP, rows, -1) for p in parts], axis=2)
    back = lax.all_to_all(sent, "dev", 0, 0, axis_index_groups=groups_of(devices), tiled=True)
    return [back[:, :, i].transpose(1, 0, 2).reshape(rows, -1) for i in range(len(parts))]


def shifted(shard, by, devices):
    pairs = [(i, i + by) for i in range(devices) if 0 <= i + by < devices]
    return lax.ppermute(shard, "dev", pairs)


def body(
    tokens,
    cotangent,
    image_lengths,
    ln1_gain,
    ln1_bias,
    qkv_weight,
    qv_bias,
    proj_weight,
    proj_bias,
    scale_attn,
    ln2_gain,
    ln2_bias,
    fc1_weight,
    fc1_bias,
    fc2_weight,
    fc2_bias,
    scale_mlp,
):
    devices = lax.axis_size("dev")
    me = lax.axis_index("dev")
    rows, width = tokens.shape
    vectors = (
        ln1_gain, ln1_bias, qv_bias, proj_bias, scale_attn, ln2_gain, ln2_bias, fc1_bias, fc2_bias, scale_mlp,
    )
    sizes = [v.shape[0] for v in vectors]
    packed = gathered(pack(vectors, 1)).astype(F32)
    gain1, shift1, bias_qv, bias_proj, layer_attn, gain2, shift2, bias_fc1, bias_fc2, layer_mlp = unpack(packed, sizes)
    w_qkv = gathered(qkv_weight)
    w_proj = gathered(proj_weight)
    w_fc1 = gathered(fc1_weight)
    w_fc2 = gathered(fc2_weight)

    span = GROUP * rows
    halo = -(-(SEQ - 1) // BK) * BK
    base = (me // GROUP) * span - halo
    places = base + halo + jnp.arange(span, dtype=jnp.int32)
    ends = jnp.cumsum(image_lengths)
    before = ends[None, :] <= places[:, None]
    begin = jnp.max(jnp.where(before, ends[None, :], 0), axis=1)
    finish = jnp.min(jnp.where(before, devices * rows, ends[None, :]), axis=1)
    seg = jnp.stack([begin - base, finish - base]).astype(jnp.int32)
    low = seg[0, ::BQ] // BK
    high = -(-seg[1, BQ - 1 :: BQ] // BK)

    x = tokens.astype(F32)
    u1, rstd1 = normalised(x)
    n1 = (u1 * gain1 + shift1).astype(BF16)
    qkv = mm(n1, w_qkv)
    q_mine = (qkv[:, :width] + bias_qv[:width]).astype(BF16)
    k_mine = qkv[:, width : 2 * width].astype(BF16)
    v_mine = (qkv[:, 2 * width :] + bias_qv[width:]).astype(BF16)
    q, k, v = to_heads([q_mine, k_mine, v_mine], devices)
    kv = jnp.concatenate([k, v], axis=1)
    left = shifted(kv[span - halo :], GROUP, devices)
    right = shifted(kv[:halo], -GROUP, devices)
    window = jnp.concatenate([left, kv, right], axis=0)
    k_win, v_win = window[:, : q.shape[1]], window[:, q.shape[1] :]
    o_heads, lse = attention_forward(low, high, seg, q, k_win, v_win)
    (o,) = to_tokens([o_heads], devices)

    branch = mm(o, w_proj) + bias_proj
    y1 = x + layer_attn * branch
    u2, rstd2 = normalised(y1)
    n2 = (u2 * gain2 + shift2).astype(BF16)
    act, slope = gelu_parts(mm(n2, w_fc1) + bias_fc1)
    act = act.astype(BF16)
    mlp = mm(act, w_fc2) + bias_fc2
    block_out = (y1 + layer_mlp * mlp).astype(BF16)

    g = cotangent.astype(F32)
    d_scale_mlp = jnp.sum(g * mlp, axis=0)
    dm = layer_mlp * g
    d_fc2_bias = jnp.sum(dm, axis=0)
    dml = dm.astype(BF16)
    d_fc2 = t_mm(act, dml)
    dz = mm_t(dml, w_fc2) * slope
    d_fc1_bias = jnp.sum(dz, axis=0)
    dzl = dz.astype(BF16)
    d_fc1 = t_mm(n2, dzl)
    dn2 = mm_t(dzl, w_fc1)
    d_gain2 = jnp.sum(dn2 * u2, axis=0)
    d_shift2 = jnp.sum(dn2, axis=0)
    dy1 = g + norm_back(u2, rstd2, dn2 * gain2)
    d_scale_attn = jnp.sum(dy1 * branch, axis=0)
    db = layer_attn * dy1
    d_proj_bias = jnp.sum(db, axis=0)
    dbl = db.astype(BF16)
    d_proj = t_mm(o, dbl)
    do = mm_t(dbl, w_proj).astype(BF16)

    (do_heads,) = to_heads([do], devices)
    dq, mid, edge = attention_backward(low, high, seg, q, k_win, v_win, o_heads, do_heads, lse, halo)
    from_right = shifted(edge[0], -GROUP, devices).astype(F32)
    from_left = shifted(edge[1], GROUP, devices).astype(F32)
    rest = span - halo
    mid = mid + jnp.pad(from_left, ((0, rest), (0, 0))) + jnp.pad(from_right, ((rest, 0), (0, 0)))
    mid = mid.astype(BF16)
    half = dq.shape[1]
    dq, dk, dv = to_tokens([dq, mid[:, :half], mid[:, half:]], devices)
    dqkv = jnp.concatenate([dq, dk, dv], axis=1)
    d_qv_bias = jnp.concatenate([jnp.sum(dq.astype(F32), axis=0), jnp.sum(dv.astype(F32), axis=0)])
    d_qkv = t_mm(n1, dqkv)
    dn1 = mm_t(dqkv, w_qkv)
    d_gain1 = jnp.sum(dn1 * u1, axis=0)
    d_shift1 = jnp.sum(dn1, axis=0)
    grad_tokens = (dy1 + norm_back(u1, rstd1, dn1 * gain1)).astype(BF16)

    small = (
        d_gain1, d_shift1, d_qv_bias, d_proj_bias, d_scale_attn, d_gain2, d_shift2, d_fc1_bias, d_fc2_bias, d_scale_mlp,
    )
    small = scattered(pack(small, devices))
    s_gain1, s_shift1, s_qv, s_proj, s_attn, s_gain2, s_shift2, s_fc1, s_fc2, s_mlp = unpack(small, sizes)
    return (
        block_out,
        grad_tokens,
        s_gain1,
        s_shift1,
        scattered(d_qkv),
        s_qv,
        scattered(d_proj),
        s_proj,
        s_attn,
        s_gain2,
        s_shift2,
        scattered(d_fc1),
        s_fc1,
        scattered(d_fc2),
        s_fc2,
        s_mlp,
    )


def solution(mesh):
    matrix, vector = P("dev", None), P("dev")
    return jax.shard_map(
        body,
        mesh=mesh,
        in_specs=(
            matrix, matrix, P(), vector, vector, matrix, vector, matrix, vector, vector, vector, vector, matrix,
            vector, matrix, vector, vector,
        ),
        out_specs=(
            matrix, matrix, vector, vector, matrix, vector, matrix, vector, vector, vector, vector, matrix, vector,
            matrix, vector, vector,
        ),
        check_vma=False,
    )
```

time: 1670 us -> 1040 us (0.62)
  matrix products: 378 us -> 90.2 us
  blocking collectives: 302 us -> 123 us
  Pallas kernels: 0 us -> 133 us
  starting transfers between devices: 151 us -> 23.8 us
  local copies, waits for them, and re-layouts: 128 us -> 15.4 us
  other arithmetic: 59.5 us -> 20.3 us
    dot_general x124 -> x12, matrix products: 378 us -> 90.2 us  [the longest x4 41.3 us: t_mm(): return jnp.einsum('td,tf->df', left, right, preferred_element_type=F32)]
    ppermute x16 -> x4, starting transfers between devices: 150 us -> 11.7 us  [shifted(): return lax.ppermute(shard, 'dev', pairs)]
    pallas_call x0 -> x2, Pallas kernels: none -> 133 us  [the longest x1 71.5 us: attention_backward(): pl.pallas_call(backward_kernel, out_shape=(jax.ShapeDtypeStruct((span, wi...]
    ppermute x16 -> x4, waiting for transfers between devices: 162 us -> 36.5 us  [shifted(): return lax.ppermute(shard, 'dev', pairs)]
    all_gather x1, blocking collectives: 155 us -> 43.8 us  [gathered(): return lax.all_gather(shard, 'dev', axis=0, tiled=True)]
    unnamed x2 -> x1, blocking collectives: 147 us -> 39 us
    all_gather x4, waiting for transfers between devices: 20.3 us -> 76.8 us  [gathered(): return lax.all_gather(shard, 'dev', axis=0, tiled=True)]
    unnamed x116 -> x50, local copies, waits for them, and re-layouts: 58.3 us -> 4.44 us
  transfers between devices with their start and end apart: 24 -> 15, of which waited for: 9 -> 12; matrix products, arithmetic and copies ran while one was open for 30% -> 10% of each run, Pallas kernels for 0% -> 13%
where the time goes in v1:
time: 1040 us; the launch traced here: 1030 us
  waiting for transfers between devices  612 us (59%)
  Pallas kernels  133 us (13%)
  blocking collectives  123 us (12%)
  matrix products  90.2 us (9%)
  starting transfers between devices  23.8 us (2%)
  other arithmetic  20.3 us (2%)
  local copies, waits for them, and re-layouts  15.4 us (1%)
  between operations  14.9 us (1%)
    reduce_scatter x4, waiting for transfers between devices, scattered(): return lax.psum_scatter(whole, 'dev', scatter_dimension=0, tiled=True)  444 us
    all_gather x4, waiting for transfers between devices, gathered(): return lax.all_gather(shard, 'dev', axis=0, tiled=True)  76.8 us
    pallas_call x1, Pallas kernels, attention_backward(): pl.pallas_call(backward_kernel, out_shape=(jax.ShapeDtypeStruct((span, wi...  71.5 us
    pallas_call x1, Pallas kernels, attention_forward(): pl.pallas_call(forward_kernel, out_shape=(jax.ShapeDtypeStruct((span, wid...  61 us
    all_gather x1, blocking collectives, gathered(): return lax.all_gather(shard, 'dev', axis=0, tiled=True)  43.8 us
    dot_general x4, matrix products, t_mm(): return jnp.einsum('td,tf->df', left, right, preferred_element_type=F32)  41.3 us
    all_to_all x1, blocking collectives, to_tokens(): lax.all_to_all(sent, 'dev', 0, 0, axis_index_groups=groups_of(devices), t...  39.9 us
    unnamed x1, blocking collectives  39 us
  transfers between devices with their start and end apart: 15, of which 12 were waited for; matrix products, arithmetic and copies ran while one was open for 10% of the time, Pallas kernels for 13%

profile of v1, /device:TPU:0, one launch (start us, length us, event | category | flops | bytes accessed | tf_op | source)
XLA Modules:
  0.0 1031.9 jit_solution(14124716443936548926)
XLA Ops:
  10.0 0.9 concatenate.23
  10.9 43.8 %all-gather = bf16[32,1,448]{2,1,0:T(2,128)(2,1)S(1)} all-gather(bf16[1,1,448]{2,1,0:T(2,128)(2,1)S(1)} %bitcast.174), channel_id=1, replica_groups=mesh['dev'=32] {'dev'}, dimensions={0}, use_global_device_ids=true | all-gather | bytes 29568 | tf_op jit(solution)/shard_map/all_gather | solution.py:239
  55.7 27.4 %all-gather.6.cloned.1.call-done = bf16[1024,3072]{1,0:T(8,128)(2,1)} async-done(((bf16[32,3072]{1,0:T(8,128)(2,1)}), bf16[1024,3072]{1,0:T(8,128)(2,1)}) %all-gather.6.cloned.1.call-update) | async-done | bytes 6291472 | tf_op jit(solution)/shard_map/all_gather | solution.py:239
  83.1 4.9 fusion.47
  89.5 1.7 maximum_bitcast_fusion
  91.1 3.8 all-to-all-start
  95.3 30.8 %all-to-all-done = bf16[8,384,3,128]{3,1,2,0:T(8,128)(2,1)S(1)} async-done(((bf16[8,384,3,128]{3,1,2,0:T(8,128)(2,1)}), bf16[8,384,3,128]{3,1,2,0:T(8,128)(2,1)S(1)}, u32[]{:S(2)}, u32[]{:S(2)}) %all-to-all-start) | async-done | bytes 2359328 | tf_op jit(solution)/shard_map/all_to_all | solution.py:262
  126.1 1.0 fusion.52
  127.2 1.5 fusion.32
  128.9 1.3 collective-permute-start.1
  130.2 4.6 collective-permute-start
  135.1 18.1 %collective-permute-done.1 = bf16[1536,256]{1,0:T(8,128)(2,1)S(1)} collective-permute-done((bf16[1536,256]{1,0:T(8,128)(2,1)}, bf16[1536,256]{1,0:T(8,128)(2,1)S(1)}, u32[]{:S(2)}, u32[]{:S(2)}) %collective-permute-start.1) | collective-permute-done | bytes 786464 | tf_op jit(solution)/shard_map/ppermute | solution.py:275
  153.2 1.3 collective-permute-done
  154.5 9.2 pad_maximum_fusion
  163.9 0.9 copy-done.2
  164.8 61.0 %attention_forward.1 = (bf16[3072,128]{1,0:T(8,128)(2,1)S(1)}, f32[8,3072]{1,0:T(8,128)S(1)}) custom-call(s32[12]{0:T(128)S(1)} %and_select_fusion.1.low, s32[12]{0:T(128)S(1)} %fusion.43.high, s32[2,3072]{1,0:T(2,128)S(1)} %pad_add_fusion.seg, bf16[3072,128]{1,0:T(8,128)(2,1)S(1)} %bitcast.143, bf16[6144,128]{1,0:T(8,128)(2,1)S(1)} %get-tuple-element.48.k_ref, ...), custom_call_target="tpu_custom_call" | custom-call | flops 9663676416 | bytes 8388608 | tf_op jit(solution)/shard_map/attention_forward/pallas_call | solution.py:140
  225.9 1.2 copy.59
  227.0 4.2 all-to-all-start.1
  231.7 13.0 %all-to-all-done.1 = bf16[8,384,1,128]{1,3,2,0:T(8,128)(2,1)S(1)} async-done(((bf16[8,384,1,128]{1,3,2,0:T(8,128)(2,1)}), bf16[8,384,1,128]{1,3,2,0:T(8,128)(2,1)S(1)}, u32[]{:S(2)}, u32[]{:S(2)}) %all-to-all-start.1) | async-done | bytes 786464 | tf_op jit(solution)/shard_map/all_to_all | solution.py:269
  244.8 0.9 copy-done.7
  245.7 4.1 fusion.49
  250.1 9.1 multiply_convert_fusion
  259.2 49.4 %all-gather.12.cloned.1.call-done = bf16[4096,1024]{1,0:T(8,128)(2,1)} async-done(((bf16[128,1024]{1,0:T(8,128)(2,1)}), bf16[4096,1024]{1,0:T(8,128)(2,1)}) %all-gather.12.cloned.1.call-update) | async-done | bytes 8388624 | tf_op jit(solution)/shard_map/all_gather | solution.py:239
  308.6 8.3 fusion.56
  316.9 8.3 multiply_reduce_fusion
  325.4 5.0 fusion.22
  330.4 1.0 fusion.29
  331.8 1.0 copy.77
  332.8 3.5 all-to-all-start.2
  336.4 4.6 fusion.39
  341.1 7.8 all-to-all-done.2
  348.8 71.5 %attention_backward.1 = (bf16[3072,128]{1,0:T(8,128)(2,1)S(1)}, f32[3072,256]{1,0:T(8,128)}, bf16[2,1536,256]{2,1,0:T(8,128)(2,1)S(1)}) custom-call(s32[12]{0:T(128)S(1)} %and_select_fusion.1.low, s32[12]{0:T(128)S(1)} %fusion.43.high, s32[2,3072]{1,0:T(2,128)S(1)} %pad_add_fusion.seg, bf16[3072,128]{1,0:T(8,128)(2,1)S(1)} %bitcast.144, ...), custom_call_target="tpu_custom_call" | custom-call | flops 24159191040 | bytes 16777216 | tf_op jit(solution)/shard_map/attention_backward/pallas_call | solution.py:165
  420.4 1.2 slice_bitcast_fusion.1
  421.6 1.3 collective-permute-start.3
  422.9 4.6 collective-permute-start.2
  427.9 15.7 %collective-permute-done.3 = bf16[1536,256]{1,0:T(8,128)(2,1)S(1)} collective-permute-done((bf16[1536,256]{1,0:T(8,128)(2,1)}, bf16[1536,256]{1,0:T(8,128)(2,1)S(1)}, u32[]{:S(2)}, u32[]{:S(2)}) %collective-permute-start.3) | collective-permute-done | bytes 786464 | tf_op jit(solution)/shard_map/ppermute | solution.py:275
  443.6 1.4 collective-permute-done.2
  445.0 2.3 add_convert_fusion
  448.4 39.9 %all_to_all.20 = bf16[8,384,3,128]{1,3,2,0:T(8,128)(2,1)S(1)} all-to-all(bf16[8,384,3,128]{1,3,2,0:T(8,128)(2,1)S(1)} %pad_maximum_fusion.1), channel_id=1, replica_groups={{0,1,2,3,4,5,6,7},{8,9,10,11,12,13,14,15},{16,17,18,19,20,21,22,23},{24..., dimensions={0} | all-to-all | bytes 4718592 | tf_op jit(solution)/shard_map/all_to_all | solution.py:269
  490.0 9.5 fusion.30
  499.6 13.7 %fusion.25 = f32[1024,4096]{1,0:T(8,128)} fusion(bf16[384,4096]{1,0:T(8,128)(2,1)} %copy-done.16, f32[384,1024]{1,0:T(8,128)} %copy-done.6, f32[1024]{0:T(1024)S(1)} %add.161, f32[1024]{0:T(1024)S(1)} %mul.186, f32[384]{0:T(512)S(1)} %add_rsqrt_fusion, f32[384]{0:T(512)S(1)} %broadcast_multiply_fusion.4), kind=kOutput, calls=%fused_computation.50 | convolution fusion | flops 3223191552 | bytes 21507072 | tf_op jit(solution)/shard_map/td,tf->df/dot_general | solution.py:213
  513.5 13.5 %fusion.36 = f32[4096,1024]{1,0:T(8,128)} fusion(bf16[384,4096]{1,0:T(8,128)(2,1)} %get-tuple-element.84, bf16[384,1024]{1,0:T(8,128)(2,1)} %param.18, f32[1024]{0:T(1024)S(1)} %mul.181), kind=kOutput, calls=%fused_computation.75 | convolution fusion | flops 3222405120 | bytes 20713472 | tf_op jit(solution)/shard_map/td,tf->df/dot_general | solution.py:213
  527.5 8.1 fusion.20
  536.4 39.0 %all-reduce.2 = f32[32,448]{1,0:T(8,128)S(1)} all-reduce(f32[32,448]{1,0:T(8,128)S(1)} %concatenate.30), channel_id=2, replica_groups=mesh['dev'=32] {'dev'}, use_global_device_ids=true, to_apply=%region_22.23.clone | all-reduce | flops 14336 | bytes 114688
  577.2 3.4 fusion.19
  580.6 71.8 %reduce-scatter.5.cloned.1.call-done = f32[32,3072]{1,0:T(8,128)} async-done(((f32[1024,3072]{1,0:T(8,128)}), f32[32,3072]{1,0:T(8,128)}) %reduce-scatter.5.cloned.1.call-update) | async-done | bytes 393232 | tf_op jit(solution)/shard_map/reduce_scatter | solution.py:243
  652.4 185.1 %reduce-scatter.9.cloned.1.call-done = f32[32,4096]{1,0:T(8,128)} async-done(((f32[1024,4096]{1,0:T(8,128)}), f32[32,4096]{1,0:T(8,128)}) %reduce-scatter.9.cloned.1.call-update) | async-done | bytes 524304 | tf_op jit(solution)/shard_map/reduce_scatter | solution.py:243
  837.5 187.3 %reduce-scatter.11.cloned.1.call-done = f32[128,1024]{1,0:T(8,128)} async-done(((f32[4096,1024]{1,0:T(8,128)}), f32[128,1024]{1,0:T(8,128)}) %reduce-scatter.11.cloned.1.call-update) | async-done | bytes 524304 | tf_op jit(solution)/shard_map/reduce_scatter | solution.py:243
  (127 shorter events, 13.9 us)
Async XLA Ops:
  7.2 48.0 %copy-start.4 = (bf16[384,1024]{1,0:T(8,128)(2,1)S(1)}, bf16[384,1024]{1,0:T(8,128)(2,1)}, u32[]{:S(2)}) copy-start(bf16[384,1024]{1,0:T(8,128)(2,1)} %param.17) | copy-start | bytes 2359300
  7.2 75.9 %all-gather.6.cloned.1.call-start = ((), (), s32[]{:S(2)}) async-start(), calls=%async_computation.8 | async-start | bytes 6488064 | tf_op jit(solution)/shard_map/all_gather | solution.py:239
  7.9 223.8 %all-gather.8.cloned.1.call-start = ((), (), s32[]{:S(2)}) async-start(), calls=%async_computation.9 | async-start | bytes 2162688 | tf_op jit(solution)/shard_map/all_gather | solution.py:239
  8.7 241.4 %all-gather.10.cloned.1.call-start = ((), (), s32[]{:S(2)}) async-start(), calls=%async_computation.10 | async-start | bytes 8650752 | tf_op jit(solution)/shard_map/all_gather | solution.py:239
  9.4 299.1 %all-gather.12.cloned.1.call-start = ((), (), s32[]{:S(2)}) async-start(), calls=%async_computation.11 | async-start | bytes 8650752 | tf_op jit(solution)/shard_map/all_gather | solution.py:239
  91.1 3.8 copy-start.21
  91.1 35.0 %all-to-all-start = ((bf16[8,384,3,128]{3,1,2,0:T(8,128)(2,1)}), bf16[8,384,3,128]{3,1,2,0:T(8,128)(2,1)S(1)}, u32[]{:S(2)}, u32[]{:S(2)}) async-start(bf16[8,384,3,128]{3,1,2,0:T(8,128)(2,1)} %maximum_bitcast_fusion), calls=%async_computation | async-start | bytes 4718592 | tf_op jit(solution)/shard_map/all_to_all | solution.py:262
  127.2 1.5 copy-start.9
  127.2 1.7 copy-start.10
  128.9 24.3 %collective-permute-start.1 = (bf16[1536,256]{1,0:T(8,128)(2,1)}, bf16[1536,256]{1,0:T(8,128)(2,1)S(1)}, u32[]{:S(2)}, u32[]{:S(2)}) collective-permute-start(bf16[1536,256]{1,0:T(8,128)(2,1)} %get-tuple-element.64), channel_id=1, source_target_pairs={{8,0},{9,1},{10,2},{11,3},{12,4},{13,5},{14,6},{15,7},{16,8},{17,9... | collective-permute-start | bytes 2359304 | tf_op jit(solution)/shard_map/ppermute | solution.py:275
  130.2 24.3 %collective-permute-start = (bf16[1536,256]{1,0:T(8,128)(2,1)}, bf16[1536,256]{1,0:T(8,128)(2,1)S(1)}, u32[]{:S(2)}, u32[]{:S(2)}) collective-permute-start(bf16[1536,256]{1,0:T(8,128)(2,1)} %get-tuple-element.63), channel_id=1, source_target_pairs={{0,8},{1,9},{2,10},{3,11},{4,12},{5,13},{6,14},{7,15},{8,16},{9,17... | collective-permute-start | bytes 2359304 | tf_op jit(solution)/shard_map/ppermute | solution.py:275
  163.7 1.1 copy-start.2
  163.9 62.0 %copy-start = (bf16[6144,128]{1,0:T(8,128)(2,1)}, bf16[6144,128]{1,0:T(8,128)(2,1)S(1)}, u32[]{:S(2)}) copy-start(bf16[6144,128]{1,0:T(8,128)(2,1)S(1)} %get-tuple-element.47.v_ref) | copy-start | bytes 4718596
  163.9 62.0 %copy-start.1 = (bf16[6144,128]{1,0:T(8,128)(2,1)}, bf16[6144,128]{1,0:T(8,128)(2,1)S(1)}, u32[]{:S(2)}) copy-start(bf16[6144,128]{1,0:T(8,128)(2,1)S(1)} %get-tuple-element.48.k_ref) | copy-start | bytes 4718596
  227.0 17.7 %all-to-all-start.1 = ((bf16[8,384,1,128]{1,3,2,0:T(8,128)(2,1)}), bf16[8,384,1,128]{1,3,2,0:T(8,128)(2,1)S(1)}, u32[]{:S(2)}, u32[]{:S(2)}) async-start(bf16[8,384,1,128]{1,3,2,0:T(8,128)(2,1)} %copy.59), calls=%async_computation.1 | async-start | bytes 1572864 | tf_op jit(solution)/shard_map/all_to_all | solution.py:269
  244.8 0.9 copy-start.7
  249.7 75.6 %copy-start.6 = (f32[384,1024]{1,0:T(8,128)}, f32[384,1024]{1,0:T(8,128)S(1)}, u32[]{:S(2)}) copy-start(f32[384,1024]{1,0:T(8,128)S(1)} %get-tuple-element.44) | copy-start | bytes 4718596
  250.0 58.5 %copy-start.19 = (bf16[384,1024]{1,0:T(8,128)(2,1)S(1)}, bf16[384,1024]{1,0:T(8,128)(2,1)}, u32[]{:S(2)}) copy-start(bf16[384,1024]{1,0:T(8,128)(2,1)} %param.18) | copy-start | bytes 2359300
  316.9 8.4 copy-start.16
  316.9 8.4 copy-start.12
  316.9 8.4 copy-start.18
  316.9 8.4 copy-start.20
  325.4 5.0 copy-start.17
  330.4 1.2 copy-start.11
  331.7 4.6 copy-start.8
  332.8 16.1 %all-to-all-start.2 = ((bf16[8,384,1,128]{3,1,2,0:T(8,128)(2,1)}), bf16[8,384,1,128]{3,1,2,0:T(8,128)(2,1)S(1)}, u32[]{:S(2)}, u32[]{:S(2)}) async-start(bf16[8,384,1,128]{3,1,2,0:T(8,128)(2,1)} %bitcast.141), calls=%async_computation.2 | async-start | bytes 1572864 | tf_op jit(solution)/shard_map/all_to_all | solution.py:262
  336.3 244.3 %reduce-scatter.7.cloned.1.call-start = ((), (), s32[]{:S(2)}) async-start(), calls=%async_computation.13 | async-start | bytes 4325376 | tf_op jit(solution)/shard_map/reduce_scatter | solution.py:243
  341.0 7.9 copy-start.3
  341.0 311.4 %reduce-scatter.5.cloned.1.call-start = ((), (), s32[]{:S(2)}) async-start(), calls=%async_computation.12 | async-start | bytes 12976128 | tf_op jit(solution)/shard_map/reduce_scatter | solution.py:243
  421.6 22.0 %collective-permute-start.3 = (bf16[1536,256]{1,0:T(8,128)(2,1)}, bf16[1536,256]{1,0:T(8,128)(2,1)S(1)}, u32[]{:S(2)}, u32[]{:S(2)}) collective-permute-start(bf16[1536,256]{1,0:T(8,128)(2,1)} %get-tuple-element.62), channel_id=1, source_target_pairs={{8,0},{9,1},{10,2},{11,3},{12,4},{13,5},{14,6},{15,7},{16,8},{17,9... | collective-permute-start | bytes 2359304 | tf_op jit(solution)/shard_map/ppermute | solution.py:275
  422.9 22.1 %collective-permute-start.2 = (bf16[1536,256]{1,0:T(8,128)(2,1)}, bf16[1536,256]{1,0:T(8,128)(2,1)S(1)}, u32[]{:S(2)}, u32[]{:S(2)}) collective-permute-start(bf16[1536,256]{1,0:T(8,128)(2,1)} %get-tuple-element.61), channel_id=1, source_target_pairs={{0,8},{1,9},{2,10},{3,11},{4,12},{5,13},{6,14},{7,15},{8,16},{9,17... | collective-permute-start | bytes 2359304 | tf_op jit(solution)/shard_map/ppermute | solution.py:275
  488.3 1.7 copy-start.5
  488.6 0.9 copy-start.13
  488.6 1.1 copy-start.14
  488.7 1.4 copy-start.15
  499.5 338.0 %reduce-scatter.9.cloned.1.call-start = ((), (), s32[]{:S(2)}) async-start(), calls=%async_computation.14 | async-start | bytes 17301504 | tf_op jit(solution)/shard_map/reduce_scatter | solution.py:243
  513.3 511.5 %reduce-scatter.11.cloned.1.call-start = ((), (), s32[]{:S(2)}) async-start(), calls=%async_computation.15 | async-start | bytes 17301504 | tf_op jit(solution)/shard_map/reduce_scatter | solution.py:243
Sparse Core Ops, SparseCore 0:
  10.9 72.1 all-gather.5
  86.0 63.3 all-gather.7
  152.2 77.4 all-gather.9
  232.5 76.0 all-gather.11
  341.1 143.2 reduce-scatter.6
  499.7 152.7 reduce-scatter.4
  655.4 182.0 reduce-scatter.8
  840.5 184.3 reduce-scatter.10

commit v2 on v1

--- a/solution.py
+++ b/solution.py
@@ -273,6 +273,166 @@
 def shifted(shard, by, devices):
     pairs = [(i, i + by) for i in range(devices) if 0 <= i + by < devices]
     return lax.ppermute(shard, "dev", pairs)
+
+
+def take(stack, index, axis):
+    return lax.dynamic_index_in_dim(stack, index, axis, keepdims=False)
+
+
+def swapped(value, bit, devices):
+    return lax.ppermute(value, "dev", [(i, i ^ bit) for i in range(devices)])
+
+
+def column_groups(devices):
+    return [list(range(first, devices, GROUP)) for first in range(GROUP)]
+
+
+def across_planes(stack, devices):
+    return lax.all_to_all(stack, "dev", 0, 0, axis_index_groups=column_groups(devices), tiled=True)
+
+
+def assemble_kernel(bits, *refs):
+    sources, (weight, vector), sem = refs[:4], refs[4:6], refs[6]
+    y, x, c = bits[0], bits[1], bits[2]
+    half = sources[0].shape[-1]
+    copies = []
+    for far in range(2):
+        for i in range(2):
+            for j in range(2):
+                a = sources[far].at[i, j]
+                b = sources[2 + far].at[j, i]
+                target = weight.at[:, y ^ j, x ^ i, c ^ far]
+                copies.append((a, target.at[:, :, :half]))
+                copies.append((b.at[:, :, : weight.shape[-1] - half], target.at[:, :, half:]))
+                copies.append((b.at[:, :, weight.shape[-1] - half :], vector.at[:, y ^ j, x ^ i, c ^ far]))
+    started = [pltpu.make_async_copy(s, t, sem.at[n]) for n, (s, t) in enumerate(copies)]
+    for copy in started:
+        copy.start()
+    for copy in started:
+        copy.wait()
+
+
+def position(me):
+    return (me // 4) % 2, (me // 2) % 2, me % 2
+
+
+def gather_by_axes(weight, extra, me, devices):
+    planes, (rows, width) = devices // GROUP, weight.shape
+    half = width // 2
+    shard = jnp.concatenate([weight, extra], axis=1)
+    stack = across_planes(jnp.broadcast_to(shard[None], (planes, *shard.shape)), devices)
+    a, b = stack[..., :half], stack[..., half:]
+    a = jnp.stack([a, swapped(a, 4, devices)])
+    b = jnp.stack([b, swapped(b, 2, devices)])
+    a = jnp.stack([a, swapped(a, 2, devices)])
+    b = jnp.stack([b, swapped(b, 4, devices)])
+    far_a, far_b = swapped(a, 1, devices), swapped(b, 1, devices)
+    anywhere = pl.BlockSpec(memory_space=pl.ANY)
+    out, vec = pl.pallas_call(
+        assemble_kernel,
+        out_shape=(
+            jax.ShapeDtypeStruct((planes, 2, 2, 2, rows, width), weight.dtype),
+            jax.ShapeDtypeStruct((planes, 2, 2, 2, rows, extra.shape[1]), weight.dtype),
+        ),
+        grid_spec=pltpu.PrefetchScalarGridSpec(
+            num_scalar_prefetch=1,
+            grid=(1,),
+            in_specs=[anywhere] * 4,
+            out_specs=[anywhere] * 2,
+            scratch_shapes=[pltpu.SemaphoreType.DMA((24,))],
+        ),
+        cost_estimate=pl.CostEstimate(flops=0, bytes_accessed=4 * devices * rows * width, transcendentals=0),
+        name="assemble",
+    )(jnp.stack(position(me)).astype(jnp.int32), a, far_a, b, far_b)
+    return out.reshape(devices * rows, width), vec.reshape(devices * rows, -1)
+
+
+def grad_kernel(bits, a_ref, b_ref, keep_ref, send_ref, a_t):
+    step = pl.program_id(0)
+    per, rows, width = keep_ref.shape
+
+    @pl.when(step == 0)
+    def _():
+        for j in range(a_ref.shape[1] // 128):
+            part = a_ref[:, j * 128 : (j + 1) * 128].astype(F32).T.astype(BF16)
+            for i in range(128 // rows):
+                owner = j * (128 // rows) + i
+                a_t[(owner % 2) ^ bits[2], owner // 2] = part[i * rows : (i + 1) * rows]
+
+    columns = 512
+    for side, out in enumerate((keep_ref, send_ref)):
+        left = a_t[side, pl.ds(step * per, per)].reshape(per * rows, -1)
+        for n in range(width // columns):
+            at = slice(n * columns, (n + 1) * columns)
+            out[:, :, at] = mm(left, b_ref[:, at]).reshape(per, rows, columns).astype(BF16)
+
+
+def weight_grad(a, b, rows, me):
+    tokens, height = a.shape
+    width = b.shape[1]
+    blocks = height // (2 * rows)
+    per = 256 // rows
+    out = jax.ShapeDtypeStruct((blocks, rows, width), BF16)
+    tile = pl.BlockSpec((per, rows, width), lambda i, *_: (i, 0, 0))
+    return pl.pallas_call(
+        grad_kernel,
+        out_shape=(out, out),
+        grid_spec=pltpu.PrefetchScalarGridSpec(
+            num_scalar_prefetch=1,
+            grid=(blocks // per,),
+            in_specs=[
+                pl.BlockSpec((tokens, height), lambda i, *_: (0, 0)),
+                pl.BlockSpec((tokens, width), lambda i, *_: (0, 0)),
+            ],
+            out_specs=[tile, tile],
+            scratch_shapes=[pltpu.VMEM((2, blocks, rows, tokens), BF16)],
+        ),
+        compiler_params=pltpu.CompilerParams(vmem_limit_bytes=48 << 20),
+        cost_estimate=pl.CostEstimate(
+            flops=2 * tokens * height * width, bytes_accessed=2 * height * width + 2 * tokens * (height + width),
+            transcendentals=0,
+        ),
+        name="weight_grad",
+    )(jnp.stack(position(me)).astype(jnp.int32), a, b)
+
+
+def scatter_by_axes(keep, send, me, devices):
+    y, x, _ = position(me)
+    blocks, rows, width = keep.shape
+    half = width // 2
+    got = swapped(send, 1, devices)
+    shape = (devices // GROUP, 2, 2, rows, width)
+    keep, got = keep.reshape(shape), got.reshape(shape)
+    columns = (slice(0, half), slice(half, width))
+
+    def first(part, index, axis):
+        return take(keep[..., part], index, axis).astype(F32) + take(got[..., part], index, axis).astype(F32)
+
+    a_got = swapped(first(columns[0], 1 - x, 2).astype(BF16), 2, devices)
+    b_got = swapped(first(columns[1], 1 - y, 1).astype(BF16), 4, devices)
+    a = (first(columns[0], x, 2) + a_got.astype(F32)).astype(BF16)
+    b = (first(columns[1], y, 1) + b_got.astype(F32)).astype(BF16)
+    a_more = swapped(take(a, 1 - y, 1), 4, devices)
+    b_more = swapped(take(b, 1 - x, 1), 2, devices)
+    a = take(a, y, 1).astype(F32) + a_more.astype(F32)
+    b = take(b, x, 1).astype(F32) + b_more.astype(F32)
+    planes = across_planes(jnp.concatenate([a, b], axis=2).astype(BF16), devices)
+    return jnp.sum(planes.astype(F32), axis=0)
+
+
+def pack_columns(vectors, rows):
+    columns = jnp.concatenate([v.reshape(-1, rows).T for v in vectors], axis=1)
+    return jnp.pad(columns, ((0, 0), (0, 128 - columns.shape[1])))
+
+
+def unpack_columns(packed, sizes, rows):
+    lines, out, at = packed[:, :16].T, [], 0
+    for size in sizes:
+        count = size // rows
+        part = lines[at : at + count].reshape(count, -1, rows)
+        out.append(part.transpose(1, 0, 2).reshape(-1))
+        at += count
+    return out
 
 
 def body(
@@ -301,9 +461,21 @@
         ln1_gain, ln1_bias, qv_bias, proj_bias, scale_attn, ln2_gain, ln2_bias, fc1_bias, fc2_bias, scale_mlp,
     )
     sizes = [v.shape[0] for v in vectors]
-    packed = gathered(pack(vectors, 1)).astype(F32)
-    gain1, shift1, bias_qv, bias_proj, layer_attn, gain2, shift2, bias_fc1, bias_fc2, layer_mlp = unpack(packed, sizes)
-    w_qkv = gathered(qkv_weight)
+    shard_rows = qkv_weight.shape[0]
+    by_axes = shard_rows % 32 == 0
+    if by_axes:
+        w_qkv, packed = gather_by_axes(qkv_weight, pack_columns(vectors, shard_rows), me, devices)
+        spread = unpack_columns(packed.astype(F32), sizes, shard_rows)
+    else:
+        w_qkv = gathered(qkv_weight)
+        spread = unpack(gathered(pack(vectors, 1)).astype(F32), sizes)
+    gain1, shift1, bias_qv, bias_proj, layer_attn, gain2, shift2, bias_fc1, bias_fc2, layer_mlp = spread
+
+    def summed(a, b, rows):
+        if by_axes:
+            return scatter_by_axes(*weight_grad(a, b, rows, me), me, devices)
+        return scattered(t_mm(a, b))
+
     w_proj = gathered(proj_weight)
     w_fc1 = gathered(fc1_weight)
     w_fc2 = gathered(fc2_weight)
@@ -350,11 +522,11 @@
     dm = layer_mlp * g
     d_fc2_bias = jnp.sum(dm, axis=0)
     dml = dm.astype(BF16)
-    d_fc2 = t_mm(act, dml)
+    d_fc2 = summed(act, dml, fc2_weight.shape[0])
     dz = mm_t(dml, w_fc2) * slope
     d_fc1_bias = jnp.sum(dz, axis=0)
     dzl = dz.astype(BF16)
-    d_fc1 = t_mm(n2, dzl)
+    d_fc1 = summed(n2, dzl, fc1_weight.shape[0])
     dn2 = mm_t(dzl, w_fc1)
     d_gain2 = jnp.sum(dn2 * u2, axis=0)
     d_shift2 = jnp.sum(dn2, axis=0)
@@ -363,7 +535,7 @@
     db = layer_attn * dy1
     d_proj_bias = jnp.sum(db, axis=0)
     dbl = db.astype(BF16)
-    d_proj = t_mm(o, dbl)
+    d_proj = scattered(t_mm(o, dbl))
     do = mm_t(dbl, w_proj).astype(BF16)
 
     (do_heads,) = to_heads([do], devices)
@@ -377,7 +549,7 @@
     dq, dk, dv = to_tokens([dq, mid[:, :half], mid[:, half:]], devices)
     dqkv = jnp.concatenate([dq, dk, dv], axis=1)
     d_qv_bias = jnp.concatenate([jnp.sum(dq.astype(F32), axis=0), jnp.sum(dv.astype(F32), axis=0)])
-    d_qkv = t_mm(n1, dqkv)
+    d_qkv = summed(n1, dqkv, shard_rows)
     dn1 = mm_t(dqkv, w_qkv)
     d_gain1 = jnp.sum(dn1 * u1, axis=0)
     d_shift1 = jnp.sum(dn1, axis=0)
@@ -386,23 +558,24 @@
     small = (
         d_gain1, d_shift1, d_qv_bias, d_proj_bias, d_scale_attn, d_gain2, d_shift2, d_fc1_bias, d_fc2_bias, d_scale_mlp,
     )
-    small = scattered(pack(small, devices))
+    small = lax.all_to_all(pack(small, devices), "dev", 0, 0, tiled=True)
+    small = jnp.sum(small, axis=0, keepdims=True)
     s_gain1, s_shift1, s_qv, s_proj, s_attn, s_gain2, s_shift2, s_fc1, s_fc2, s_mlp = unpack(small, sizes)
     return (
         block_out,
         grad_tokens,
         s_gain1,
         s_shift1,
-        scattered(d_qkv),
+        d_qkv,
         s_qv,
-        scattered(d_proj),
+        d_proj,
         s_proj,
         s_attn,
         s_gain2,
         s_shift2,
-        scattered(d_fc1),
+        d_fc1,
         s_fc1,
-        scattered(d_fc2),
+        d_fc2,
         s_fc2,
         s_mlp,
     )

time: 1040 us -> 854 us (0.82)
  waiting for transfers between devices: 612 us -> 254 us
  Pallas kernels: 133 us -> 336 us
  blocking collectives: 123 us -> 15 us
  starting transfers between devices: 23.8 us -> 84.7 us
  matrix products: 90.2 us -> 51.6 us
  local copies, waits for them, and re-layouts: 15.4 us -> 46.8 us
  other arithmetic: 20.3 us -> 40.9 us
    reduce_scatter x4 -> x1, waiting for transfers between devices: 444 us -> 0.01 us  [scattered(): return lax.psum_scatter(whole, 'dev', scatter_dimension=0, tiled=True)]
    pallas_call x0 -> x4, Pallas kernels: none -> 222 us  [the longest x1 201 us: gather_by_axes(): pl.pallas_call(assemble_kernel, out_shape=(jax.ShapeDtypeStruct((planes,...]
    ppermute x0 -> x21, waiting for transfers between devices: none -> 126 us  [swapped(): return lax.ppermute(value, 'dev', [(i, i ^ bit) for i in range(devices)])]
    all_gather x4 -> x3, waiting for transfers between devices: 76.8 us -> 0.04 us  [gathered(): return lax.all_gather(shard, 'dev', axis=0, tiled=True)]
    all_to_all x0 -> x5, waiting for transfers between devices: none -> 53.1 us  [the longest x4 53.1 us: across_planes(): lax.all_to_all(stack, 'dev', 0, 0, axis_index_groups=column_groups(device...]
    all_gather x1 -> x0, blocking collectives: 43.8 us -> none  [gathered(): return lax.all_gather(shard, 'dev', axis=0, tiled=True)]
    unnamed x1 -> x0, blocking collectives: 39 us -> none
    dot_general x4 -> x1, matrix products: 41.3 us -> 4.64 us  [t_mm(): return jnp.einsum('td,tf->df', left, right, preferred_element_type=F32)]
  transfers between devices with their start and end apart: 15 -> 37, of which waited for: 12 -> 21; matrix products, arithmetic and copies ran while one was open for 10% -> 12% of each run, Pallas kernels for 13% -> 33%
where the time goes in v2:
time: 854 us; the launch traced here: 843 us
  Pallas kernels  336 us (39%)
  waiting for transfers between devices  254 us (30%)
  starting transfers between devices  84.7 us (10%)
  matrix products  51.6 us (6%)
  local copies, waits for them, and re-layouts  46.8 us (5%)
  other arithmetic  40.9 us (5%)
  blocking collectives  15 us (2%)
  between operations  15 us (2%)
    pallas_call x1, Pallas kernels, gather_by_axes(): pl.pallas_call(assemble_kernel, out_shape=(jax.ShapeDtypeStruct((planes,...  201 us
    ppermute x21, waiting for transfers between devices, swapped(): return lax.ppermute(value, 'dev', [(i, i ^ bit) for i in range(devices)])  126 us
    pallas_call x1, Pallas kernels, attention_backward(): pl.pallas_call(backward_kernel, out_shape=(jax.ShapeDtypeStruct((span, wi...  61.5 us
    all_to_all x4, waiting for transfers between devices, across_planes(): lax.all_to_all(stack, 'dev', 0, 0, axis_index_groups=column_groups(device...  53.1 us
    pallas_call x1, Pallas kernels, attention_forward(): pl.pallas_call(forward_kernel, out_shape=(jax.ShapeDtypeStruct((span, wid...  51.8 us
    all_to_all x1, waiting for transfers between devices, to_heads(): lax.all_to_all(sent, 'dev', 0, 0, axis_index_groups=groups_of(devices), t...  29.1 us
    ppermute x4, waiting for transfers between devices, shifted(): return lax.ppermute(shard, 'dev', pairs)  28.2 us
    dot_general x4, matrix products, mm(): return jnp.dot(left, right, preferred_element_type=F32)  26.4 us
  transfers between devices with their start and end apart: 37, of which 21 were waited for; matrix products, arithmetic and copies ran while one was open for 12% of the time, Pallas kernels for 33%

profile of v2, /device:TPU:0, one launch (start us, length us, event | category | flops | bytes accessed | tf_op | source)
XLA Modules:
  0.0 843.1 jit_solution(10156818211987338208)
XLA Ops:
  13.6 6.3 all-to-all-start
  20.7 21.5 %all-to-all-done = bf16[4,32,3200]{2,1,0:T(8,128)(2,1)S(1)} async-done(((bf16[4,32,3200]{2,1,0:T(8,128)(2,1)}), bf16[4,32,3200]{2,1,0:T(8,128)(2,1)S(1)}, u32[]{:S(2)}, u32[]{:S(2)}) %all-to-all-start) | async-done | bytes 819232 | tf_op jit(solution)/shard_map/all_to_all | solution.py:291
  45.4 9.5 %collective-permute-done.3 = bf16[4,32,1664]{2,1,0:T(8,128)(2,1)S(1)} collective-permute-done((bf16[4,32,1664]{2,1,0:T(8,128)(2,1)S(1)}, bf16[4,32,1664]{2,1,0:T(8,128)(2,1)S(1)}, u32[]{:S(2)}, u32[]{:S(2)}) %collective-permute-start.3) | collective-permute-done | bytes 426016 | tf_op jit(solution)/shard_map/ppermute | solution.py:283
  58.3 19.5 %collective-permute-done.4 = bf16[2,4,32,1664]{3,2,1,0:T(8,128)(2,1)S(1)} collective-permute-done((bf16[2,4,32,1664]{3,2,1,0:T(8,128)(2,1)S(1)}, bf16[2,4,32,1664]{3,2,1,0:T(8,128)(2,1)S(1)}, u32[]{:S(2)}, u32[]{:S(2)}) %collective-permute-start.4) | collective-permute-done | bytes 852000 | tf_op jit(solution)/shard_map/ppermute | solution.py:283
  81.0 3.2 collective-permute-done.2.refs_1_
  84.3 200.5 %assemble.1 = (bf16[4,2,2,2,32,3072]{5,4,3,2,1,0:T(8,128)(2,1)}, bf16[4,2,2,2,32,128]{5,4,3,2,1,0:T(8,128)(2,1)}) custom-call(s32[3]{0:T(128)} %pad_add_fusion.1.bits, bf16[2,2,4,32,1536]{4,3,2,1,0:T(8,128)(2,1)} %pad_maximum_fusion.3.refs_0_, bf16[2,2,4,32,1536]{4,3,2,1,0:T(8,128)(2,1)} %collective-permute-done.2.refs_1_, ...), custom_call_target="tpu_custom_call" | custom-call | bytes 12582912 | tf_op jit(solution)/shard_map/assemble/pallas_call | solution.py:331
  286.6 5.0 fusion.73
  294.7 4.5 all-to-all-start.1
  299.6 29.1 %all-to-all-done.1 = bf16[8,384,3,128]{3,1,2,0:T(8,128)(2,1)} async-done(((bf16[8,384,3,128]{3,1,2,0:T(8,128)(2,1)}), bf16[8,384,3,128]{3,1,2,0:T(8,128)(2,1)}, u32[]{:S(2)}, u32[]{:S(2)}) %all-to-all-start.1) | async-done | bytes 2359328 | tf_op jit(solution)/shard_map/all_to_all | solution.py:262
  328.7 2.7 fusion.69
  334.0 5.5 collective-permute-start.6
  339.8 11.3 %collective-permute-done.7 = bf16[1536,256]{1,0:T(8,128)(2,1)S(1)} collective-permute-done((bf16[1536,256]{1,0:T(8,128)(2,1)}, bf16[1536,256]{1,0:T(8,128)(2,1)S(1)}, u32[]{:S(2)}, u32[]{:S(2)}) %collective-permute-start.7) | collective-permute-done | bytes 786464 | tf_op jit(solution)/shard_map/ppermute | solution.py:275
  355.5 51.8 %attention_forward.1 = (bf16[3072,128]{1,0:T(8,128)(2,1)S(1)}, f32[8,3072]{1,0:T(8,128)S(1)}) custom-call(s32[12]{0:T(128)S(1)} %get-tuple-element.139.low, s32[12]{0:T(128)S(1)} %get-tuple-element.140.high, s32[2,3072]{1,0:T(2,128)S(1)} %pad_add_fusion.seg, bf16[3072,128]{1,0:T(8,128)(2,1)S(1)} %bitcast.274, bf16[6144,128]{1,0:T(8,128)(2,1)S(1)} %get-tuple-element.78.k_ref, ...), custom_call_target="tpu_custom_call" | custom-call | flops 9663676416 | bytes 8388608 | tf_op jit(solution)/shard_map/attention_forward/pallas_call | solution.py:140
  408.4 5.2 all-to-all-start.2
  415.3 11.0 %all-to-all-done.2 = bf16[8,384,1,128]{1,3,2,0:T(8,128)(2,1)S(1)} async-done(((bf16[8,384,1,128]{1,3,2,0:T(8,128)(2,1)}), bf16[8,384,1,128]{1,3,2,0:T(8,128)(2,1)S(1)}, u32[]{:S(2)}, u32[]{:S(2)}) %all-to-all-start.2) | async-done | bytes 786464 | tf_op jit(solution)/shard_map/all_to_all | solution.py:269
  426.2 4.1 fusion.60
  431.8 8.8 %multiply_convert_fusion = (bf16[384,4096]{1,0:T(8,128)(2,1)}, f32[384,4096]{1,0:T(8,128)}) fusion(f32[4096]{0:T(1024)S(1)} %add.339, bf16[384,1024]{1,0:T(8,128)(2,1)S(1)} %add_convert_fusion.5.a_ref, bf16[1024,4096]{1,0:T(8,128)(2,1)} %all-gather.6.cloned.1.call-done), kind=kOutput, calls=%fused_computation.6 | convolution fusion | flops 3230662656 | bytes 18628608 | tf_op jit(solution)/shard_map/dot_general | solution.py:205
  440.6 8.7 %fusion.61 = (f32[4096]{0:T(1024)S(1)}, bf16[384,4096]{1,0:T(8,128)(2,1)S(1)}) fusion(f32[384,4096]{1,0:T(8,128)} %get-tuple-element.135, bf16[384,1024]{1,0:T(8,128)(2,1)S(1)} %fusion.18.b_ref, bf16[4096,1024]{1,0:T(8,128)(2,1)} %all-gather.8.cloned.1.call-done), kind=kOutput, calls=%fused_computation.193 | convolution fusion | flops 3238522880 | bytes 18628608 | tf_op jit(solution)/shard_map/tf,df->td/dot_general | solution.py:209
  449.4 3.9 multiply_reduce_fusion
  453.3 8.6 %fusion.28 = (f32[1024]{0:T(1024)S(1)}, f32[1024]{0:T(1024)S(1)}, bf16[384,1024]{1,0:T(8,128)(2,1)}, f32[1024]{0:T(1024)S(1)}, f32[1024]{0:T(1024)S(1)}, /*index=5*/f32[384,1024]{1,0:T(8,128)S(1)}) fusion(bf16[384,1024]{1,0:T(8,128)(2,1)S(1)} %copy-done.40, f32[1024]{0:T(1024)S(1)} %bitcast.326, f32[1024]{0:T(1024)S(1)} %bitcast.319, ...), kind=kOutput, calls=%fused_computation.53 | convolution fusion | flops 3229478912 | bytes 19437568 | tf_op jit(solution)/shard_map/dot_general | solution.py:205
  463.2 15.0 %all_to_all.49 = bf16[8,384,1,128]{3,1,2,0:T(8,128)(2,1)S(1)} all-to-all(bf16[8,384,1,128]{3,1,2,0:T(8,128)(2,1)S(1)} %bitcast.295), channel_id=1, replica_groups={{0,1,2,3,4,5,6,7},{8,9,10,11,12,13,14,15},{16,17,18,19,20,21,22,23},{24..., dimensions={0} | all-to-all | bytes 1572864 | tf_op jit(solution)/shard_map/all_to_all | solution.py:262
  478.2 61.5 %attention_backward.1 = (bf16[3072,128]{1,0:T(8,128)(2,1)S(1)}, f32[3072,256]{1,0:T(8,128)}, bf16[2,1536,256]{2,1,0:T(8,128)(2,1)S(1)}) custom-call(s32[12]{0:T(128)S(1)} %get-tuple-element.139.low, s32[12]{0:T(128)S(1)} %get-tuple-element.140.high, s32[2,3072]{1,0:T(2,128)S(1)} %pad_add_fusion.seg, bf16[3072,128]{1,0:T(8,128)(2,1)S(1)} %bitcast.275, ...), custom_call_target="tpu_custom_call" | custom-call | flops 24159191040 | bytes 16777216 | tf_op jit(solution)/shard_map/attention_backward/pallas_call | solution.py:165
  542.3 14.8 %collective-permute-start.8 = (bf16[1536,256]{1,0:T(8,128)(2,1)}, bf16[1536,256]{1,0:T(8,128)(2,1)}, u32[]{:S(2)}, u32[]{:S(2)}) collective-permute-start(bf16[1536,256]{1,0:T(8,128)(2,1)} %get-tuple-element.103), channel_id=1, source_target_pairs={{0,8},{1,9},{2,10},{3,11},{4,12},{5,13},{6,14},{7,15},{8,16},{9,17... | collective-permute-start | bytes 2359304 | tf_op jit(solution)/shard_map/ppermute | solution.py:275
  557.2 14.3 %collective-permute-done.9 = bf16[1536,256]{1,0:T(8,128)(2,1)S(1)} collective-permute-done((bf16[1536,256]{1,0:T(8,128)(2,1)}, bf16[1536,256]{1,0:T(8,128)(2,1)S(1)}, u32[]{:S(2)}, u32[]{:S(2)}) %collective-permute-start.9) | collective-permute-done | bytes 786464 | tf_op jit(solution)/shard_map/ppermute | solution.py:275
  572.7 2.4 add_convert_fusion
  576.9 4.5 all-to-all-start.4
  581.9 4.6 fusion.52
  589.6 7.4 weight_grad.4
  597.3 8.4 weight_grad.5
  613.6 3.6 all-to-all-done.4
  620.1 6.9 fusion.26
  629.8 5.5 all-to-all-start.5
  635.3 6.0 weight_grad.3
  644.9 2.9 fusion.65
  653.2 2.7 fusion.63
  659.0 19.5 %collective-permute-done.18 = bf16[4,2,32,2048]{3,2,1,0:T(8,128)(2,1)S(1)} collective-permute-done((bf16[4,2,32,2048]{3,2,1,0:T(8,128)(2,1)S(1)}, bf16[4,2,32,2048]{3,2,1,0:T(8,128)(2,1)S(1)}, u32[]{:S(2)}, u32[]{:S(2)}) %collective-permute-start.18) | collective-permute-done | bytes 1048608 | tf_op jit(solution)/shard_map/ppermute | solution.py:283
  681.4 23.1 %collective-permute-done.23 = bf16[4,2,128,512]{3,2,1,0:T(8,128)(2,1)S(1)} collective-permute-done((bf16[4,2,128,512]{3,2,1,0:T(8,128)(2,1)S(1)}, bf16[4,2,128,512]{3,2,1,0:T(8,128)(2,1)S(1)}, u32[]{:S(2)}, u32[]{:S(2)}) %collective-permute-start.23) | collective-permute-done | bytes 1048608 | tf_op jit(solution)/shard_map/ppermute | solution.py:283
  707.4 13.3 %collective-permute-done.21 = bf16[4,2,128,512]{3,2,0,1:T(8,128)(2,1)S(1)} collective-permute-done((bf16[4,2,128,512]{3,2,0,1:T(8,128)(2,1)S(1)}, bf16[4,2,128,512]{3,2,0,1:T(8,128)(2,1)S(1)}, u32[]{:S(2)}, u32[]{:S(2)}) %collective-permute-start.21) | collective-permute-done | bytes 1048608 | tf_op jit(solution)/shard_map/ppermute | solution.py:283
  724.1 20.5 %collective-permute-done.24 = bf16[4,128,512]{2,1,0:T(8,128)(2,1)S(1)} collective-permute-done((bf16[4,128,512]{2,1,0:T(8,128)(2,1)S(1)}, bf16[4,128,512]{2,1,0:T(8,128)(2,1)S(1)}, u32[]{:S(2)}, u32[]{:S(2)}) %collective-permute-start.24) | collective-permute-done | bytes 524320 | tf_op jit(solution)/shard_map/ppermute | solution.py:283
  751.8 4.2 all-to-all-start.7
  761.4 8.6 %collective-permute-done.13 = bf16[4,2,32,1536]{3,2,1,0:T(8,128)(2,1)} collective-permute-done((bf16[4,2,32,1536]{3,2,1,0:T(8,128)(2,1)}, bf16[4,2,32,1536]{3,2,1,0:T(8,128)(2,1)}, u32[]{:S(2)}, u32[]{:S(2)}) %collective-permute-start.13) | collective-permute-done | bytes 786464 | tf_op jit(solution)/shard_map/ppermute | solution.py:283
  774.3 7.4 all-to-all-done.7
  781.7 3.5 all-to-all-start.8
  788.8 8.2 collective-permute-done.12
  798.1 12.4 %all-to-all-done.8 = bf16[4,128,1024]{2,1,0:T(8,128)(2,1)S(1)} async-done(((bf16[4,128,1024]{2,1,0:T(8,128)(2,1)}), bf16[4,128,1024]{2,1,0:T(8,128)(2,1)S(1)}, u32[]{:S(2)}, u32[]{:S(2)}) %all-to-all-start.8) | async-done | bytes 1048608 | tf_op jit(solution)/shard_map/all_to_all | solution.py:291
  810.5 4.2 all-to-all-start.6
  814.7 2.9 fusion.25
  822.5 11.8 %all-to-all-done.6 = bf16[4,32,3072]{2,1,0:T(8,128)(2,1)} async-done(((bf16[4,32,3072]{2,1,0:T(8,128)(2,1)}), bf16[4,32,3072]{2,1,0:T(8,128)(2,1)}, u32[]{:S(2)}, u32[]{:S(2)}) %all-to-all-start.6) | async-done | bytes 786464 | tf_op jit(solution)/shard_map/all_to_all | solution.py:291
  (266 shorter events, 107.2 us)
Async XLA Ops:
  7.2 408.1 %all-gather.4.cloned.1.call-start = ((), (), s32[]{:S(2)}) async-start(), calls=%async_computation.10 | async-start | bytes 2162688 | tf_op jit(solution)/shard_map/all_gather | solution.py:239
  7.9 423.9 %all-gather.6.cloned.1.call-start = ((), (), s32[]{:S(2)}) async-start(), calls=%async_computation.11 | async-start | bytes 8650752 | tf_op jit(solution)/shard_map/all_gather | solution.py:239
  13.6 28.5 %all-to-all-start = ((bf16[4,32,3200]{2,1,0:T(8,128)(2,1)}), bf16[4,32,3200]{2,1,0:T(8,128)(2,1)S(1)}, u32[]{:S(2)}, u32[]{:S(2)}) async-start(bf16[4,32,3200]{2,1,0:T(8,128)(2,1)} %broadcast_in_dim.24), calls=%async_computation | async-start | bytes 1638400 | tf_op jit(solution)/shard_map/all_to_all | solution.py:291
  19.9 420.6 %all-gather.8.cloned.1.call-start = ((), (), s32[]{:S(2)}) async-start(), calls=%async_computation.12 | async-start | bytes 8650752 | tf_op jit(solution)/shard_map/all_gather | solution.py:239
  42.2 12.7 %collective-permute-start.3 = (bf16[4,32,1664]{2,1,0:T(8,128)(2,1)S(1)}, bf16[4,32,1664]{2,1,0:T(8,128)(2,1)S(1)}, u32[]{:S(2)}, u32[]{:S(2)}) collective-permute-start(bf16[4,32,1664]{2,1,0:T(8,128)(2,1)S(1)} %get-tuple-element.110), channel_id=1, source_target_pairs={{0,2},{1,3},{2,0},{3,1},{4,6},{5,7},{6,4},{7,5},{8,10},{9,11},{10,... | collective-permute-start | bytes 1277960 | tf_op jit(solution)/shard_map/ppermute | solution.py:283
  43.8 12.8 %collective-permute-start = (bf16[4,32,1536]{2,1,0:T(8,128)(2,1)S(1)}, bf16[4,32,1536]{2,1,0:T(8,128)(2,1)S(1)}, u32[]{:S(2)}, u32[]{:S(2)}) collective-permute-start(bf16[4,32,1536]{2,1,0:T(8,128)(2,1)S(1)} %get-tuple-element.112), channel_id=1, source_target_pairs={{0,4},{1,5},{2,6},{3,7},{4,0},{5,1},{6,2},{7,3},{8,12},{9,13},{10,... | collective-permute-start | bytes 1179656 | tf_op jit(solution)/shard_map/ppermute | solution.py:283
  55.0 22.8 %collective-permute-start.4 = (bf16[2,4,32,1664]{3,2,1,0:T(8,128)(2,1)S(1)}, bf16[2,4,32,1664]{3,2,1,0:T(8,128)(2,1)S(1)}, u32[]{:S(2)}, u32[]{:S(2)}) collective-permute-start(bf16[2,4,32,1664]{3,2,1,0:T(8,128)(2,1)S(1)} %get-tuple-element.108), channel_id=1, source_target_pairs={{0,4},{1,5},{2,6},{3,7},{4,0},{5,1},{6,2},{7,3},{8,12},{9,13},{10,... | collective-permute-start | bytes 2555912 | tf_op jit(solution)/shard_map/ppermute | solution.py:283
  56.7 21.4 %collective-permute-start.1 = (bf16[2,4,32,1536]{3,2,1,0:T(8,128)(2,1)S(1)}, bf16[2,4,32,1536]{3,2,1,0:T(8,128)(2,1)S(1)}, u32[]{:S(2)}, u32[]{:S(2)}) collective-permute-start(bf16[2,4,32,1536]{3,2,1,0:T(8,128)(2,1)S(1)} %get-tuple-element.114), channel_id=1, source_target_pairs={{0,2},{1,3},{2,0},{3,1},{4,6},{5,7},{6,4},{7,5},{8,10},{9,11},{10,... | collective-permute-start | bytes 2359304 | tf_op jit(solution)/shard_map/ppermute | solution.py:283
  78.0 6.3 collective-permute-start.5
  79.4 4.9 collective-permute-start.2
  294.7 34.0 %all-to-all-start.1 = ((bf16[8,384,3,128]{3,1,2,0:T(8,128)(2,1)}), bf16[8,384,3,128]{3,1,2,0:T(8,128)(2,1)}, u32[]{:S(2)}, u32[]{:S(2)}) async-start(bf16[8,384,3,128]{3,1,2,0:T(8,128)(2,1)} %maximum_bitcast_fusion), calls=%async_computation.1 | async-start | bytes 4718592 | tf_op jit(solution)/shard_map/all_to_all | solution.py:262
  332.7 18.4 %collective-permute-start.7 = (bf16[1536,256]{1,0:T(8,128)(2,1)}, bf16[1536,256]{1,0:T(8,128)(2,1)S(1)}, u32[]{:S(2)}, u32[]{:S(2)}) collective-permute-start(bf16[1536,256]{1,0:T(8,128)(2,1)} %get-tuple-element.106), channel_id=1, source_target_pairs={{8,0},{9,1},{10,2},{11,3},{12,4},{13,5},{14,6},{15,7},{16,8},{17,9... | collective-permute-start | bytes 2359304 | tf_op jit(solution)/shard_map/ppermute | solution.py:275
  334.0 18.4 %collective-permute-start.6 = (bf16[1536,256]{1,0:T(8,128)(2,1)}, bf16[1536,256]{1,0:T(8,128)(2,1)}, u32[]{:S(2)}, u32[]{:S(2)}) collective-permute-start(bf16[1536,256]{1,0:T(8,128)(2,1)} %get-tuple-element.105), channel_id=1, source_target_pairs={{0,8},{1,9},{2,10},{3,11},{4,12},{5,13},{6,14},{7,15},{8,16},{9,17... | collective-permute-start | bytes 2359304 | tf_op jit(solution)/shard_map/ppermute | solution.py:275
  354.5 52.7 %copy-start = (bf16[6144,128]{1,0:T(8,128)(2,1)}, bf16[6144,128]{1,0:T(8,128)(2,1)S(1)}, u32[]{:S(2)}) copy-start(bf16[6144,128]{1,0:T(8,128)(2,1)S(1)} %get-tuple-element.77.v_ref) | copy-start | bytes 4718596
  354.5 52.7 %copy-start.1 = (bf16[6144,128]{1,0:T(8,128)(2,1)}, bf16[6144,128]{1,0:T(8,128)(2,1)S(1)}, u32[]{:S(2)}) copy-start(bf16[6144,128]{1,0:T(8,128)(2,1)S(1)} %get-tuple-element.78.k_ref) | copy-start | bytes 4718596
  408.4 17.8 %all-to-all-start.2 = ((bf16[8,384,1,128]{1,3,2,0:T(8,128)(2,1)}), bf16[8,384,1,128]{1,3,2,0:T(8,128)(2,1)S(1)}, u32[]{:S(2)}, u32[]{:S(2)}) async-start(bf16[8,384,1,128]{1,3,2,0:T(8,128)(2,1)} %copy.119), calls=%async_computation.2 | async-start | bytes 1572864 | tf_op jit(solution)/shard_map/all_to_all | solution.py:269
  440.6 8.8 %copy-start.41 = (bf16[1024,4096]{1,0:T(8,128)(2,1)S(1)}, bf16[1024,4096]{1,0:T(8,128)(2,1)}, u32[]{:S(2)}) copy-start(bf16[1024,4096]{1,0:T(8,128)(2,1)} %all-gather.6.cloned.1.call-done) | copy-start | bytes 25165828
  461.9 16.3 %copy-start.21 = (f32[384,1024]{1,0:T(8,128)}, f32[384,1024]{1,0:T(8,128)S(1)}, u32[]{:S(2)}) copy-start(f32[384,1024]{1,0:T(8,128)S(1)} %get-tuple-element.96) | copy-start | bytes 4718596
  462.9 15.3 %copy-start.3 = (bf16[8,384,1,128]{3,1,2,0:T(8,128)(2,1)S(1)}, bf16[8,384,1,128]{3,1,2,0:T(8,128)(2,1)}, u32[]{:S(2)}) copy-start(bf16[8,384,1,128]{3,1,2,0:T(8,128)(2,1)} %get-tuple-element.84) | copy-start | bytes 2359300
  541.0 30.4 %collective-permute-start.9 = (bf16[1536,256]{1,0:T(8,128)(2,1)}, bf16[1536,256]{1,0:T(8,128)(2,1)S(1)}, u32[]{:S(2)}, u32[]{:S(2)}) collective-permute-start(bf16[1536,256]{1,0:T(8,128)(2,1)} %get-tuple-element.104), channel_id=1, source_target_pairs={{8,0},{9,1},{10,2},{11,3},{12,4},{13,5},{14,6},{15,7},{16,8},{17,9... | collective-permute-start | bytes 2359304 | tf_op jit(solution)/shard_map/ppermute | solution.py:275
  542.3 30.4 %collective-permute-start.8 = (bf16[1536,256]{1,0:T(8,128)(2,1)}, bf16[1536,256]{1,0:T(8,128)(2,1)}, u32[]{:S(2)}, u32[]{:S(2)}) collective-permute-start(bf16[1536,256]{1,0:T(8,128)(2,1)} %get-tuple-element.103), channel_id=1, source_target_pairs={{0,8},{1,9},{2,10},{3,11},{4,12},{5,13},{6,14},{7,15},{8,16},{9,17... | collective-permute-start | bytes 2359304 | tf_op jit(solution)/shard_map/ppermute | solution.py:275
  576.9 40.3 %all-to-all-start.4 = ((bf16[8,384,3,128]{3,1,2,0:T(8,128)(2,1)}), bf16[8,384,3,128]{3,1,2,0:T(8,128)(2,1)}, u32[]{:S(2)}, u32[]{:S(2)}) async-start(bf16[8,384,3,128]{3,1,2,0:T(8,128)(2,1)} %pad_maximum_fusion.1), calls=%async_computation.4 | async-start | bytes 4718592 | tf_op jit(solution)/shard_map/all_to_all | solution.py:269
  581.4 254.9 %reduce-scatter.2.cloned.1.call-start = ((), (), s32[]{:S(2)}) async-start(), calls=%async_computation.13 | async-start | bytes 4325376 | tf_op jit(solution)/shard_map/reduce_scatter | solution.py:243
  597.0 48.0 %collective-permute-start.15 = (bf16[16,32,4096]{2,1,0:T(8,128)(2,1)}, bf16[16,32,4096]{2,1,0:T(8,128)(2,1)}, u32[]{:S(2)}, u32[]{:S(2)}) collective-permute-start(bf16[16,32,4096]{2,1,0:T(8,128)(2,1)} %get-tuple-element.39), channel_id=1, source_target_pairs={{0,1},{1,0},{2,3},{3,2},{4,5},{5,4},{6,7},{7,6},{8,9},{9,8},{10,11... | collective-permute-start | bytes 12582920 | tf_op jit(solution)/shard_map/ppermute | solution.py:283
  605.7 47.6 %collective-permute-start.20 = (bf16[16,128,1024]{2,1,0:T(8,128)(2,1)}, bf16[16,128,1024]{2,1,0:T(8,128)(2,1)}, u32[]{:S(2)}, u32[]{:S(2)}) collective-permute-start(bf16[16,128,1024]{2,1,0:T(8,128)(2,1)} %get-tuple-element.41), channel_id=1, source_target_pairs={{0,1},{1,0},{2,3},{3,2},{4,5},{5,4},{6,7},{7,6},{8,9},{9,8},{10,11... | collective-permute-start | bytes 12582920 | tf_op jit(solution)/shard_map/ppermute | solution.py:283
  629.8 122.0 %all-to-all-start.5 = ((f32[32,1,448]{2,1,0:T(1,128)}), f32[32,1,448]{2,1,0:T(1,128)S(1)}, u32[]{:S(2)}, u32[]{:S(2)}) async-start(f32[32,1,448]{2,1,0:T(1,128)} %all_to_all.35), calls=%async_computation.5 | async-start | bytes 131072 | tf_op jit(solution)/shard_map/all_to_all | solution.py:561
  641.2 107.5 %collective-permute-start.10 = (bf16[16,32,3072]{2,1,0:T(8,128)(2,1)}, bf16[16,32,3072]{2,1,0:T(8,128)(2,1)S(1)}, u32[]{:S(2)}, u32[]{:S(2)}) collective-permute-start(bf16[16,32,3072]{2,1,0:T(8,128)(2,1)} %get-tuple-element.37), channel_id=1, source_target_pairs={{0,1},{1,0},{2,3},{3,2},{4,5},{5,4},{6,7},{7,6},{8,9},{9,8},{10,11... | collective-permute-start | bytes 9437192 | tf_op jit(solution)/shard_map/ppermute | solution.py:283
  648.3 30.3 %collective-permute-start.18 = (bf16[4,2,32,2048]{3,2,1,0:T(8,128)(2,1)S(1)}, bf16[4,2,32,2048]{3,2,1,0:T(8,128)(2,1)S(1)}, u32[]{:S(2)}, u32[]{:S(2)}) collective-permute-start(bf16[4,2,32,2048]{3,2,1,0:T(8,128)(2,1)S(1)} %fusion.37), channel_id=1, source_target_pairs={{0,4},{1,5},{2,6},{3,7},{4,0},{5,1},{6,2},{7,3},{8,12},{9,13},{10,... | collective-permute-start | bytes 3145736 | tf_op jit(solution)/shard_map/ppermute | solution.py:283
  651.6 70.6 %collective-permute-start.16 = (bf16[4,2,32,2048]{3,2,0,1:T(8,128)(2,1)S(1)}, bf16[4,2,32,2048]{3,2,0,1:T(8,128)(2,1)S(1)}, u32[]{:S(2)}, u32[]{:S(2)}) collective-permute-start(bf16[4,2,32,2048]{3,2,0,1:T(8,128)(2,1)S(1)} %fusion.35), channel_id=1, source_target_pairs={{0,2},{1,3},{2,0},{3,1},{4,6},{5,7},{6,4},{7,5},{8,10},{9,11},{10,... | collective-permute-start | bytes 3145736 | tf_op jit(solution)/shard_map/ppermute | solution.py:283
  656.4 48.1 %collective-permute-start.23 = (bf16[4,2,128,512]{3,2,1,0:T(8,128)(2,1)S(1)}, bf16[4,2,128,512]{3,2,1,0:T(8,128)(2,1)S(1)}, u32[]{:S(2)}, u32[]{:S(2)}) collective-permute-start(bf16[4,2,128,512]{3,2,1,0:T(8,128)(2,1)S(1)} %fusion.38), channel_id=1, source_target_pairs={{0,4},{1,5},{2,6},{3,7},{4,0},{5,1},{6,2},{7,3},{8,12},{9,13},{10,... | collective-permute-start | bytes 3145736 | tf_op jit(solution)/shard_map/ppermute | solution.py:283
  658.6 62.2 %collective-permute-start.21 = (bf16[4,2,128,512]{3,2,0,1:T(8,128)(2,1)S(1)}, bf16[4,2,128,512]{3,2,0,1:T(8,128)(2,1)S(1)}, u32[]{:S(2)}, u32[]{:S(2)}) collective-permute-start(bf16[4,2,128,512]{3,2,0,1:T(8,128)(2,1)S(1)} %fusion.36), channel_id=1, source_target_pairs={{0,2},{1,3},{2,0},{3,1},{4,6},{5,7},{6,4},{7,5},{8,10},{9,11},{10,... | collective-permute-start | bytes 3145736 | tf_op jit(solution)/shard_map/ppermute | solution.py:283
  679.1 41.7 %copy-start.30 = (bf16[4,2,1,128,512]{4,3,2,1,0:T(8,128)(2,1)S(1)}, bf16[4,2,1,128,512]{4,3,2,1,0:T(8,128)(2,1)}, u32[]{:S(2)}) copy-start(bf16[4,2,1,128,512]{4,3,2,1,0:T(8,128)(2,1)} %get-tuple-element.85) | copy-start | bytes 3145732
  679.1 67.3 %collective-permute-start.19 = (bf16[4,32,2048]{2,1,0:T(8,128)(2,1)S(1)}, bf16[4,32,2048]{2,1,0:T(8,128)(2,1)S(1)}, u32[]{:S(2)}, u32[]{:S(2)}) collective-permute-start(bf16[4,32,2048]{2,1,0:T(8,128)(2,1)S(1)} %dynamic-slice_bitcast_fusion.2), channel_id=1, source_target_pairs={{0,2},{1,3},{2,0},{3,1},{4,6},{5,7},{6,4},{7,5},{8,10},{9,11},{10,... | collective-permute-start | bytes 1572872 | tf_op jit(solution)/shard_map/ppermute | solution.py:283
  705.1 39.5 %collective-permute-start.24 = (bf16[4,128,512]{2,1,0:T(8,128)(2,1)S(1)}, bf16[4,128,512]{2,1,0:T(8,128)(2,1)S(1)}, u32[]{:S(2)}, u32[]{:S(2)}) collective-permute-start(bf16[4,128,512]{2,1,0:T(8,128)(2,1)S(1)} %dynamic-slice_bitcast_fusion), channel_id=1, source_target_pairs={{0,2},{1,3},{2,0},{3,1},{4,6},{5,7},{6,4},{7,5},{8,10},{9,11},{10,... | collective-permute-start | bytes 1572872 | tf_op jit(solution)/shard_map/ppermute | solution.py:283
  721.3 24.2 %collective-permute-start.22 = (bf16[4,128,512]{2,1,0:T(8,128)(2,1)S(1)}, bf16[4,128,512]{2,1,0:T(8,128)(2,1)S(1)}, u32[]{:S(2)}, u32[]{:S(2)}) collective-permute-start(bf16[4,128,512]{2,1,0:T(8,128)(2,1)S(1)} %dynamic-slice_bitcast_fusion.1), channel_id=1, source_target_pairs={{0,4},{1,5},{2,6},{3,7},{4,0},{5,1},{6,2},{7,3},{8,12},{9,13},{10,... | collective-permute-start | bytes 1572872 | tf_op jit(solution)/shard_map/ppermute | solution.py:283
  722.9 24.6 %collective-permute-start.17 = (bf16[4,32,2048]{2,1,0:T(8,128)(2,1)S(1)}, bf16[4,32,2048]{2,1,0:T(8,128)(2,1)S(1)}, u32[]{:S(2)}, u32[]{:S(2)}) collective-permute-start(bf16[4,32,2048]{2,1,0:T(8,128)(2,1)S(1)} %dynamic-slice_bitcast_fusion.3), channel_id=1, source_target_pairs={{0,4},{1,5},{2,6},{3,7},{4,0},{5,1},{6,2},{7,3},{8,12},{9,13},{10,... | collective-permute-start | bytes 1572872 | tf_op jit(solution)/shard_map/ppermute | solution.py:283
  751.3 18.7 %collective-permute-start.13 = (bf16[4,2,32,1536]{3,2,1,0:T(8,128)(2,1)}, bf16[4,2,32,1536]{3,2,1,0:T(8,128)(2,1)}, u32[]{:S(2)}, u32[]{:S(2)}) collective-permute-start(bf16[4,2,32,1536]{3,2,1,0:T(8,128)(2,1)} %fusion.44), channel_id=1, source_target_pairs={{0,4},{1,5},{2,6},{3,7},{4,0},{5,1},{6,2},{7,3},{8,12},{9,13},{10,... | collective-permute-start | bytes 2359304 | tf_op jit(solution)/shard_map/ppermute | solution.py:283
  751.8 30.0 %all-to-all-start.7 = ((bf16[4,32,4096]{2,1,0:T(8,128)(2,1)}), bf16[4,32,4096]{2,1,0:T(8,128)(2,1)}, u32[]{:S(2)}, u32[]{:S(2)}) async-start(bf16[4,32,4096]{2,1,0:T(8,128)(2,1)} %pad_maximum_fusion.4), calls=%async_computation.8 | async-start | bytes 2097152 | tf_op jit(solution)/shard_map/all_to_all | solution.py:291
  757.3 12.7 %copy-start.24 = (bf16[4,2,2,32,1536]{4,3,2,1,0:T(8,128)(2,1)S(1)}, bf16[4,2,2,32,1536]{4,3,2,1,0:T(8,128)(2,1)}, u32[]{:S(2)}) copy-start(bf16[4,2,2,32,1536]{4,3,2,1,0:T(8,128)(2,1)} %copy-done.23) | copy-start | bytes 4718596
  758.4 26.9 %collective-permute-start.11 = (bf16[4,2,32,1536]{3,2,0,1:T(8,128)(2,1)}, bf16[4,2,32,1536]{3,2,0,1:T(8,128)(2,1)}, u32[]{:S(2)}, u32[]{:S(2)}) collective-permute-start(bf16[4,2,32,1536]{3,2,0,1:T(8,128)(2,1)} %fusion.43), channel_id=1, source_target_pairs={{0,2},{1,3},{2,0},{3,1},{4,6},{5,7},{6,4},{7,5},{8,10},{9,11},{10,... | collective-permute-start | bytes 2359304 | tf_op jit(solution)/shard_map/ppermute | solution.py:283
  772.3 13.0 %copy-start.31 = (bf16[4,2,1,32,1536]{4,3,2,1,0:T(8,128)(2,1)S(1)}, bf16[4,2,1,32,1536]{4,3,2,1,0:T(8,128)(2,1)}, u32[]{:S(2)}) copy-start(bf16[4,2,1,32,1536]{4,3,2,1,0:T(8,128)(2,1)} %get-tuple-element.97) | copy-start | bytes 2359300
  772.3 13.0 %copy-start.33 = (bf16[4,2,1,32,1536]{4,3,2,1,0:T(8,128)(2,1)S(1)}, bf16[4,2,1,32,1536]{4,3,2,1,0:T(8,128)(2,1)}, u32[]{:S(2)}) copy-start(bf16[4,2,1,32,1536]{4,3,2,1,0:T(8,128)(2,1)} %get-tuple-element.99) | copy-start | bytes 2359300
  773.1 14.6 %collective-permute-start.14 = (bf16[4,32,1536]{2,1,0:T(8,128)(2,1)}, bf16[4,32,1536]{2,1,0:T(8,128)(2,1)}, u32[]{:S(2)}, u32[]{:S(2)}) collective-permute-start(bf16[4,32,1536]{2,1,0:T(8,128)(2,1)} %dynamic-slice_bitcast_fusion.4), channel_id=1, source_target_pairs={{0,2},{1,3},{2,0},{3,1},{4,6},{5,7},{6,4},{7,5},{8,10},{9,11},{10,... | collective-permute-start | bytes 1179656 | tf_op jit(solution)/shard_map/ppermute | solution.py:283
  781.7 28.7 %all-to-all-start.8 = ((bf16[4,128,1024]{2,1,0:T(8,128)(2,1)}), bf16[4,128,1024]{2,1,0:T(8,128)(2,1)S(1)}, u32[]{:S(2)}, u32[]{:S(2)}) async-start(bf16[4,128,1024]{2,1,0:T(8,128)(2,1)} %pad_maximum_fusion.5), calls=%async_computation.9 | async-start | bytes 2097152 | tf_op jit(solution)/shard_map/all_to_all | solution.py:291
  786.9 10.1 %collective-permute-start.12 = (bf16[4,32,1536]{2,1,0:T(8,128)(2,1)S(1)}, bf16[4,32,1536]{2,1,0:T(8,128)(2,1)S(1)}, u32[]{:S(2)}, u32[]{:S(2)}) collective-permute-start(bf16[4,32,1536]{2,1,0:T(8,128)(2,1)S(1)} %dynamic-slice_bitcast_fusion.5), channel_id=1, source_target_pairs={{0,4},{1,5},{2,6},{3,7},{4,0},{5,1},{6,2},{7,3},{8,12},{9,13},{10,... | collective-permute-start | bytes 1179656 | tf_op jit(solution)/shard_map/ppermute | solution.py:283
  788.8 25.9 %copy-start.13 = (bf16[384,1024]{1,0:T(8,128)(2,1)S(1)}, bf16[384,1024]{1,0:T(8,128)(2,1)}, u32[]{:S(2)}) copy-start(bf16[384,1024]{1,0:T(8,128)(2,1)} %param.17) | copy-start | bytes 2359300
  788.8 25.9 %copy-start.22 = (f32[384,1024]{1,0:T(8,128)S(1)}, f32[384,1024]{1,0:T(8,128)}, u32[]{:S(2)}) copy-start(f32[384,1024]{1,0:T(8,128)} %copy-done.21) | copy-start | bytes 4718596
  810.5 23.9 %all-to-all-start.6 = ((bf16[4,32,3072]{2,1,0:T(8,128)(2,1)}), bf16[4,32,3072]{2,1,0:T(8,128)(2,1)}, u32[]{:S(2)}, u32[]{:S(2)}) async-start(bf16[4,32,3072]{2,1,0:T(8,128)(2,1)} %pad_maximum_fusion.9), calls=%async_computation.6 | async-start | bytes 1572864 | tf_op jit(solution)/shard_map/all_to_all | solution.py:291
  (32 other events, 114.5 us)
Sparse Core Ops, SparseCore 0:
  10.9 71.0 all-gather.3
  84.8 76.2 all-gather.5
  164.0 76.0 all-gather.7
  587.2 146.3 reduce-scatter.1

commit v3 on v1

--- a/solution.py
+++ b/solution.py
@@ -273,6 +273,189 @@
 def shifted(shard, by, devices):
     pairs = [(i, i + by) for i in range(devices) if 0 <= i + by < devices]
     return lax.ppermute(shard, "dev", pairs)
+
+
+def take(stack, index, axis):
+    return lax.dynamic_index_in_dim(stack, index, axis, keepdims=False)
+
+
+def swapped(value, bit, devices):
+    return lax.ppermute(value, "dev", [(i, i ^ bit) for i in range(devices)])
+
+
+def across_planes(stack, devices):
+    columns = [list(range(first, devices, GROUP)) for first in range(GROUP)]
+    return lax.all_to_all(stack, "dev", 0, 0, axis_index_groups=columns, tiled=True)
+
+
+def in_plane(stack, devices):
+    return lax.all_to_all(stack, "dev", 0, 0, axis_index_groups=groups_of(devices), tiled=True)
+
+
+def position(me):
+    return (me // 4) % 2, (me // 2) % 2, me % 2
+
+
+def qkv_kernel(bits, near_a, far_a, near_b, far_b, gain, shift, weight, bias, n1_ref, q_ref, k_ref, v_ref):
+    far = pl.program_id(0) >= 4
+    left = jnp.where(far, far_a[0, 0], near_a[0, 0])
+    right = jnp.where(far, far_b[0, 0], near_b[0, 0])
+    unit, _ = normalised(jnp.concatenate([left, right], axis=1).astype(F32))
+    n1 = (unit * gain[...] + shift[...]).astype(BF16)
+    n1_ref[...] = n1
+    out = (mm(n1, weight[...]) + bias[...]).astype(BF16)
+    third = out.shape[1] // 3
+    q_ref[...] = out[:, :third]
+    k_ref[...] = out[:, third : 2 * third]
+    v_ref[...] = out[:, 2 * third :]
+
+
+def plane_qkv(tokens, gain, shift, weight, bias, me, devices):
+    rows, width = tokens.shape
+    half, third = width // 2, weight.shape[1] // 3
+    a, b = tokens[:, :half], tokens[:, half:]
+    a = jnp.stack([a, swapped(a, 4, devices)])
+    b = jnp.stack([b, swapped(b, 2, devices)])
+    a = jnp.stack([a, swapped(a, 2, devices)])
+    b = jnp.stack([b, swapped(b, 4, devices)])
+    far_a, far_b = swapped(a, 1, devices), swapped(b, 1, devices)
+
+    def near_at(s, swap):
+        i, j = (s // 2) % 2, s % 2
+        i, j = jnp.where(s < 4, i, 1), jnp.where(s < 4, j, 1)
+        return (j, i, 0, 0) if swap else (i, j, 0, 0)
+
+    def far_at(s, swap):
+        i, j = (s // 2) % 2, s % 2
+        i, j = jnp.where(s < 4, 0, i), jnp.where(s < 4, 0, j)
+        return (j, i, 0, 0) if swap else (i, j, 0, 0)
+
+    def place(s, bits):
+        return ((bits[0] ^ (s % 2)) * 4 + (bits[1] ^ ((s // 2) % 2)) * 2 + (bits[2] ^ (s // 4)), 0)
+
+    piece = (1, 1, rows, half)
+    line = pl.BlockSpec((1, width), lambda s, bits: (0, 0))
+    span = GROUP * rows
+    return pl.pallas_call(
+        qkv_kernel,
+        out_shape=(
+            jax.ShapeDtypeStruct((span, width), BF16),
+            jax.ShapeDtypeStruct((span, third), BF16),
+            jax.ShapeDtypeStruct((span, third), BF16),
+            jax.ShapeDtypeStruct((span, third), BF16),
+        ),
+        grid_spec=pltpu.PrefetchScalarGridSpec(
+            num_scalar_prefetch=1,
+            grid=(GROUP,),
+            in_specs=[
+                pl.BlockSpec(piece, lambda s, bits: near_at(s, False)),
+                pl.BlockSpec(piece, lambda s, bits: far_at(s, False)),
+                pl.BlockSpec(piece, lambda s, bits: near_at(s, True)),
+                pl.BlockSpec(piece, lambda s, bits: far_at(s, True)),
+                line,
+                line,
+                pl.BlockSpec(weight.shape, lambda s, bits: (0, 0)),
+                pl.BlockSpec((1, 3 * third), lambda s, bits: (0, 0)),
+            ],
+            out_specs=[pl.BlockSpec((rows, width), place)] + [pl.BlockSpec((rows, third), place)] * 3,
+        ),
+        compiler_params=pltpu.CompilerParams(vmem_limit_bytes=40 << 20),
+        cost_estimate=pl.CostEstimate(flops=30 << 28, bytes_accessed=16 << 20, transcendentals=0),
+        name="plane_qkv",
+    )(
+        jnp.stack(position(me)).astype(jnp.int32), a, far_a, b, far_b, gain[None], shift[None], weight, bias[None],
+    )
+
+
+def by_parity(transposed, parity, rows):
+    blocks = transposed.reshape(-1, 2, rows, transposed.shape[1])
+    even, odd = (blocks[:, s].reshape(-1, transposed.shape[1]) for s in range(2))
+    return jnp.where(parity == 0, even, odd), jnp.where(parity == 0, odd, even)
+
+
+def turned(value):
+    return value.astype(F32).T.astype(BF16)
+
+
+def mlp_kernel(
+    bits, n2_ref, dml_ref, f1_ref, f2_ref, bias, mlp_ref, dn2_ref, db_ref, keep1, send1, keep2, send2, n2_t
+):
+    step = pl.program_id(0)
+    rows = keep1.shape[1]
+
+    @pl.when(step == 0)
+    def _():
+        mlp_ref[...] = jnp.zeros_like(mlp_ref)
+        dn2_ref[...] = jnp.zeros_like(dn2_ref)
+        n2_t[0], n2_t[1] = by_parity(turned(n2_ref[...]), bits[2], rows)
+
+    n2, dml, f1, f2 = n2_ref[...], dml_ref[...], f1_ref[...], f2_ref[...]
+    act, slope = gelu_parts(mm(n2, f1) + bias[...])
+    act = act.astype(BF16)
+    mlp_ref[...] += mm(act, f2)
+    dz = lax.dot_general(dml, f2, NT, preferred_element_type=F32) * slope
+    db_ref[...] = jnp.sum(dz, axis=0, keepdims=True)
+    dz = dz.astype(BF16)
+    dn2_ref[...] += lax.dot_general(dz, f1, NT, preferred_element_type=F32)
+    for side, out in enumerate((keep1, send1)):
+        out[...] = mm(n2_t[side], dz).astype(BF16).reshape(out.shape)
+    for part, out in zip(by_parity(turned(act), bits[2], rows), (keep2, send2)):
+        out[...] = mm(part, dml).astype(BF16).reshape(out.shape)
+
+
+def mlp_all(n2, dml, big, bias, me, shard_rows):
+    tokens, width = n2.shape
+    hidden, owners = bias.shape[0], width // shard_rows
+    size = width // 2
+    steps = hidden // size
+    whole = pl.BlockSpec((tokens, width), lambda s, bits: (0, 0))
+    first = pl.BlockSpec((owners // 2, shard_rows, size), lambda s, bits: (0, 0, s))
+    second = pl.BlockSpec((owners // 4, shard_rows, width), lambda s, bits: (s % 2, 0, s // 2))
+    line = pl.BlockSpec((1, size), lambda s, bits: (0, s))
+    grads = jax.ShapeDtypeStruct((owners // 2, shard_rows, hidden), BF16)
+    total = jax.ShapeDtypeStruct((tokens, width), F32)
+    blocks = hidden // width
+    return pl.pallas_call(
+        mlp_kernel,
+        out_shape=(total, total, jax.ShapeDtypeStruct((1, hidden), F32), grads, grads, grads, grads),
+        grid_spec=pltpu.PrefetchScalarGridSpec(
+            num_scalar_prefetch=1,
+            grid=(steps,),
+            in_specs=[
+                whole,
+                whole,
+                pl.BlockSpec((width, size), lambda s, bits: (0, s)),
+                pl.BlockSpec((size, width), lambda s, bits: (s % 2, blocks + s // 2)),
+                line,
+            ],
+            out_specs=[whole, whole, line, first, first, second, second],
+            scratch_shapes=[pltpu.VMEM((2, width // 2, tokens), BF16)],
+        ),
+        compiler_params=pltpu.CompilerParams(vmem_limit_bytes=52 << 20),
+        cost_estimate=pl.CostEstimate(
+            flops=12 * tokens * width * hidden, bytes_accessed=8 * width * hidden, transcendentals=2 * tokens * hidden
+        ),
+        name="mlp_all",
+    )(jnp.stack(position(me)).astype(jnp.int32), n2, dml, big, big, bias[None])
+
+
+def grad_kernel(bits, a_ref, b_ref, keep_ref, send_ref):
+    for part, out in zip(by_parity(turned(a_ref[...]), bits[2], keep_ref.shape[1]), (keep_ref, send_ref)):
+        out[...] = mm(part, b_ref[...]).astype(BF16).reshape(out.shape)
+
+
+def weight_grad(a, b, rows, me):
+    out = jax.ShapeDtypeStruct((a.shape[1] // (2 * rows), rows, b.shape[1]), BF16)
+    return pl.pallas_call(
+        grad_kernel,
+        out_shape=(out, out),
+        grid_spec=pltpu.PrefetchScalarGridSpec(num_scalar_prefetch=1, grid=(1,)),
+        compiler_params=pltpu.CompilerParams(vmem_limit_bytes=40 << 20),
+        cost_estimate=pl.CostEstimate(
+            flops=2 * a.size * b.shape[1], bytes_accessed=2 * (a.size + b.size + 2 * out.size), transcendentals=0
+        ),
+        name="weight_grad",
+    )(jnp.stack(position(me)).astype(jnp.int32), a, b)
 
 
 def body(
@@ -301,12 +484,30 @@
         ln1_gain, ln1_bias, qv_bias, proj_bias, scale_attn, ln2_gain, ln2_bias, fc1_bias, fc2_bias, scale_mlp,
     )
     sizes = [v.shape[0] for v in vectors]
-    packed = gathered(pack(vectors, 1)).astype(F32)
-    gain1, shift1, bias_qv, bias_proj, layer_attn, gain2, shift2, bias_fc1, bias_fc2, layer_mlp = unpack(packed, sizes)
-    w_qkv = gathered(qkv_weight)
-    w_proj = gathered(proj_weight)
-    w_fc1 = gathered(fc1_weight)
-    w_fc2 = gathered(fc2_weight)
+    shard_rows, hidden = qkv_weight.shape[0], fc1_weight.shape[1]
+    by_axes = shard_rows % 32 == 0
+    blocks = hidden // width
+    packed = pack(vectors, 1)
+    packed = lax.all_to_all(jnp.broadcast_to(packed, (devices, packed.shape[1])), "dev", 0, 0, tiled=True)
+    spread = unpack(packed.astype(F32), sizes)
+    gain1, shift1, bias_qv, bias_proj, layer_attn, gain2, shift2, bias_fc1, bias_fc2, layer_mlp = spread
+    slab = qkv_weight.reshape(shard_rows, 3, GROUP, -1).transpose(2, 0, 1, 3).reshape(GROUP, shard_rows, -1)
+    slab = in_plane(slab, devices).reshape(1, GROUP * shard_rows, -1)
+    slab = across_planes(jnp.broadcast_to(slab, (devices // GROUP, *slab.shape[1:])), devices)
+    slab = slab.reshape(width, -1)
+    if by_axes:
+        first = fc1_weight.reshape(shard_rows, devices, blocks, shard_rows).transpose(0, 2, 1, 3)
+        second = fc2_weight.reshape(blocks, shard_rows, width).transpose(1, 0, 2)
+        big = jnp.concatenate(
+            [first.reshape(shard_rows, hidden), second.reshape(shard_rows, hidden), proj_weight], axis=1
+        )
+        big = gathered(big)
+        w_proj = big[:, 2 * hidden :]
+    else:
+        w_proj, big = gathered(proj_weight), gathered(fc1_weight)
+        w_fc2 = gathered(fc2_weight)
+    qkv_late, big = lax.optimization_barrier((qkv_weight, big))
+    w_qkv = gathered(qkv_late)
 
     span = GROUP * rows
     halo = -(-(SEQ - 1) // BK) * BK
@@ -322,12 +523,16 @@
 
     x = tokens.astype(F32)
     u1, rstd1 = normalised(x)
-    n1 = (u1 * gain1 + shift1).astype(BF16)
-    qkv = mm(n1, w_qkv)
-    q_mine = (qkv[:, :width] + bias_qv[:width]).astype(BF16)
-    k_mine = qkv[:, width : 2 * width].astype(BF16)
-    v_mine = (qkv[:, 2 * width :] + bias_qv[width:]).astype(BF16)
-    q, k, v = to_heads([q_mine, k_mine, v_mine], devices)
+    heads_width = width // GROUP
+    mine = (me % GROUP) * heads_width
+    bias = jnp.concatenate(
+        [
+            lax.dynamic_slice(bias_qv, (mine,), (heads_width,)),
+            jnp.zeros((heads_width,), F32),
+            lax.dynamic_slice(bias_qv, (width + mine,), (heads_width,)),
+        ]
+    )
+    n1, q, k, v = plane_qkv(tokens, gain1, shift1, slab, bias, me, devices)
     kv = jnp.concatenate([k, v], axis=1)
     left = shifted(kv[span - halo :], GROUP, devices)
     right = shifted(kv[:halo], -GROUP, devices)
@@ -340,22 +545,26 @@
     y1 = x + layer_attn * branch
     u2, rstd2 = normalised(y1)
     n2 = (u2 * gain2 + shift2).astype(BF16)
-    act, slope = gelu_parts(mm(n2, w_fc1) + bias_fc1)
-    act = act.astype(BF16)
-    mlp = mm(act, w_fc2) + bias_fc2
-    block_out = (y1 + layer_mlp * mlp).astype(BF16)
-
     g = cotangent.astype(F32)
-    d_scale_mlp = jnp.sum(g * mlp, axis=0)
     dm = layer_mlp * g
     d_fc2_bias = jnp.sum(dm, axis=0)
     dml = dm.astype(BF16)
-    d_fc2 = t_mm(act, dml)
-    dz = mm_t(dml, w_fc2) * slope
-    d_fc1_bias = jnp.sum(dz, axis=0)
-    dzl = dz.astype(BF16)
-    d_fc1 = t_mm(n2, dzl)
-    dn2 = mm_t(dzl, w_fc1)
+    if by_axes:
+        bias_hidden = bias_fc1.reshape(devices, blocks, shard_rows).transpose(1, 0, 2).reshape(-1)
+        mlp, dn2, d_fc1_bias, keep1, send1, keep2, send2 = mlp_all(n2, dml, big, bias_hidden, me, shard_rows)
+        d_fc1_bias = d_fc1_bias.reshape(blocks, devices, shard_rows).transpose(1, 0, 2).reshape(-1)
+    else:
+        act, slope = gelu_parts(mm(n2, big) + bias_fc1)
+        act = act.astype(BF16)
+        mlp = mm(act, w_fc2)
+        dz = mm_t(dml, w_fc2) * slope
+        d_fc1_bias = jnp.sum(dz, axis=0)
+        dz = dz.astype(BF16)
+        dn2 = mm_t(dz, big)
+        d_fc1, d_fc2 = scattered(t_mm(n2, dz)), scattered(t_mm(act, dml))
+    mlp = mlp + bias_fc2
+    block_out = (y1 + layer_mlp * mlp).astype(BF16)
+    d_scale_mlp = jnp.sum(g * mlp, axis=0)
     d_gain2 = jnp.sum(dn2 * u2, axis=0)
     d_shift2 = jnp.sum(dn2, axis=0)
     dy1 = g + norm_back(u2, rstd2, dn2 * gain2)
@@ -363,21 +572,65 @@
     db = layer_attn * dy1
     d_proj_bias = jnp.sum(db, axis=0)
     dbl = db.astype(BF16)
-    d_proj = t_mm(o, dbl)
     do = mm_t(dbl, w_proj).astype(BF16)
+
+    if by_axes:
+        y, x, _ = position(me)
+        keep3, send3 = weight_grad(o, dbl, shard_rows, me)
+        got1, got2, got3 = (swapped(s, 1, devices) for s in (send1, send2, send3))
+        do, got1, got2, got3 = lax.optimization_barrier((do, got1, got2, got3))
+        view = (devices // GROUP, 2, 2, shard_rows)
+        own1, own2, own3 = (s.reshape(*view, -1) for s in (keep1, keep2, keep3))
+        got1, got2, got3 = (s.reshape(*view, -1) for s in (got1, got2, got3))
+        cut = width // 2
+
+        def part(index, axis, which):
+            cols = slice(0, cut) if which == 0 else slice(cut, width)
+            pairs = ((own1, got1), (own2, got2))[which], (own3[..., cols], got3[..., cols])
+            both = [take(m, index, axis).astype(F32) + take(n, index, axis).astype(F32) for m, n in pairs]
+            return jnp.concatenate(both, axis=-1).astype(BF16)
+
+        out_a, out_b = part(1 - x, 2, 0), part(1 - y, 1, 1)
+        do, out_a, out_b = lax.optimization_barrier((do, out_a, out_b))
+        in_a, in_b = swapped(out_a, 2, devices), swapped(out_b, 4, devices)
+    else:
+        d_proj = scattered(t_mm(o, dbl))
 
     (do_heads,) = to_heads([do], devices)
     dq, mid, edge = attention_backward(low, high, seg, q, k_win, v_win, o_heads, do_heads, lse, halo)
+    if by_axes:
+        dq, mid, edge, in_a, in_b = lax.optimization_barrier((dq, mid, edge, in_a, in_b))
+        sum_a = (part(x, 2, 0).astype(F32) + in_a.astype(F32)).astype(BF16)
+        sum_b = (part(y, 1, 1).astype(F32) + in_b.astype(F32)).astype(BF16)
+        in_a = swapped(take(sum_a, 1 - y, 1), 4, devices)
+        in_b = swapped(take(sum_b, 1 - x, 1), 2, devices)
     from_right = shifted(edge[0], -GROUP, devices).astype(F32)
     from_left = shifted(edge[1], GROUP, devices).astype(F32)
     rest = span - halo
     mid = mid + jnp.pad(from_left, ((0, rest), (0, 0))) + jnp.pad(from_right, ((rest, 0), (0, 0)))
     mid = mid.astype(BF16)
-    half = dq.shape[1]
-    dq, dk, dv = to_tokens([dq, mid[:, :half], mid[:, half:]], devices)
-    dqkv = jnp.concatenate([dq, dk, dv], axis=1)
+    d_heads = jnp.concatenate([dq, mid], axis=1)
+    if by_axes:
+        d_heads, in_a, in_b = lax.optimization_barrier((d_heads, in_a, in_b))
+        sum_a = take(sum_a, y, 1).astype(F32) + in_a.astype(F32)
+        sum_b = take(sum_b, x, 1).astype(F32) + in_b.astype(F32)
+        planes = across_planes(jnp.concatenate([sum_a, sum_b], axis=-1).astype(BF16), devices)
+    dqkv = in_plane(d_heads.reshape(GROUP, rows, -1), devices).reshape(GROUP, rows, 3, -1)
+    dqkv = dqkv.transpose(1, 2, 0, 3).reshape(rows, 3 * width)
+    dq, dv = dqkv[:, :width], dqkv[:, 2 * width :]
+    d_qkv = t_mm(n1, d_heads).astype(BF16).reshape(devices // GROUP, GROUP, shard_rows, -1)
+    d_qkv = jnp.sum(across_planes(d_qkv, devices).astype(F32), axis=0)
+    d_qkv = in_plane(d_qkv, devices).reshape(GROUP, shard_rows, 3, -1)
+    d_qkv = d_qkv.transpose(1, 2, 0, 3).reshape(shard_rows, 3 * width)
+    if by_axes:
+        sums = jnp.sum(planes.astype(F32), axis=0)
+        d_fc1 = sums[:, :hidden].reshape(shard_rows, blocks, devices, shard_rows).transpose(0, 2, 1, 3)
+        d_fc1 = d_fc1.reshape(shard_rows, hidden)
+        at = hidden + cut
+        d_fc2 = sums[:, at : at + hidden].reshape(shard_rows, blocks, width).transpose(1, 0, 2)
+        d_fc2 = d_fc2.reshape(blocks * shard_rows, width)
+        d_proj = jnp.concatenate([sums[:, hidden:at], sums[:, at + hidden :]], axis=1)
     d_qv_bias = jnp.concatenate([jnp.sum(dq.astype(F32), axis=0), jnp.sum(dv.astype(F32), axis=0)])
-    d_qkv = t_mm(n1, dqkv)
     dn1 = mm_t(dqkv, w_qkv)
     d_gain1 = jnp.sum(dn1 * u1, axis=0)
     d_shift1 = jnp.sum(dn1, axis=0)
@@ -386,23 +639,24 @@
     small = (
         d_gain1, d_shift1, d_qv_bias, d_proj_bias, d_scale_attn, d_gain2, d_shift2, d_fc1_bias, d_fc2_bias, d_scale_mlp,
     )
-    small = scattered(pack(small, devices))
+    small = lax.all_to_all(pack(small, devices), "dev", 0, 0, tiled=True)
+    small = jnp.sum(small, axis=0, keepdims=True)
     s_gain1, s_shift1, s_qv, s_proj, s_attn, s_gain2, s_shift2, s_fc1, s_fc2, s_mlp = unpack(small, sizes)
     return (
         block_out,
         grad_tokens,
         s_gain1,
         s_shift1,
-        scattered(d_qkv),
+        d_qkv,
         s_qv,
-        scattered(d_proj),
+        d_proj,
         s_proj,
         s_attn,
         s_gain2,
         s_shift2,
-        scattered(d_fc1),
+        d_fc1,
         s_fc1,
-        scattered(d_fc2),
+        d_fc2,
         s_fc2,
         s_mlp,
     )

time: 1040 us -> 609 us (0.59)
  waiting for transfers between devices: 612 us -> 212 us
  blocking collectives: 123 us -> 35.7 us
  matrix products: 90.2 us -> 18.9 us
  starting transfers between devices: 23.8 us -> 67.3 us
  local copies, waits for them, and re-layouts: 15.4 us -> 50 us
  other arithmetic: 20.3 us -> 46.6 us
  Pallas kernels: 133 us -> 156 us
    reduce_scatter x4 -> x0, waiting for transfers between devices: 444 us -> none  [scattered(): return lax.psum_scatter(whole, 'dev', scatter_dimension=0, tiled=True)]
    all_to_all x0 -> x6, waiting for transfers between devices: none -> 116 us  [the longest x2 77 us: across_planes(): lax.all_to_all(stack, 'dev', 0, 0, axis_index_groups=columns, tiled=True)]
    all_gather x4 -> x2, waiting for transfers between devices: 76.8 us -> 0.02 us  [gathered(): return lax.all_gather(shard, 'dev', axis=0, tiled=True)]
    all_gather x1 -> x0, blocking collectives: 43.8 us -> none  [gathered(): return lax.all_gather(shard, 'dev', axis=0, tiled=True)]
    pallas_call x0 -> x3, Pallas kernels: none -> 42.8 us  [the longest x1 29.7 us: mlp_all(): pl.pallas_call(mlp_kernel, out_shape=(total, total, jax.ShapeDtypeStruct(...]
    unnamed x1 -> x0, blocking collectives: 39 us -> none
    dot_general x4 -> x1, matrix products: 41.3 us -> 3.46 us  [t_mm(): return jnp.einsum('td,tf->df', left, right, preferred_element_type=F32)]
    ppermute x0 -> x13, waiting for transfers between devices: none -> 37 us  [swapped(): return lax.ppermute(value, 'dev', [(i, i ^ bit) for i in range(devices)])]
  transfers between devices with their start and end apart: 15 -> 27, of which waited for: 12 -> 17; matrix products, arithmetic and copies ran while one was open for 10% -> 15% of each run, Pallas kernels for 13% -> 21%
where the time goes in v3:
time: 609 us; the launch traced here: 602 us
  waiting for transfers between devices  212 us (35%)
  Pallas kernels  156 us (26%)
  starting transfers between devices  67.3 us (11%)
  local copies, waits for them, and re-layouts  50 us (8%)
  other arithmetic  46.6 us (8%)
  blocking collectives  35.7 us (6%)
  matrix products  18.9 us (3%)
  between operations  15.8 us (3%)
    all_to_all x2, waiting for transfers between devices, across_planes(): lax.all_to_all(stack, 'dev', 0, 0, axis_index_groups=columns, tiled=True)  77 us
    pallas_call x1, Pallas kernels, attention_backward(): pl.pallas_call(backward_kernel, out_shape=(jax.ShapeDtypeStruct((span, wi...  60.9 us
    pallas_call x1, Pallas kernels, attention_forward(): pl.pallas_call(forward_kernel, out_shape=(jax.ShapeDtypeStruct((span, wid...  51.8 us
    ppermute x4, waiting for transfers between devices, shifted(): return lax.ppermute(shard, 'dev', pairs)  46.3 us
    ppermute x13, waiting for transfers between devices, swapped(): return lax.ppermute(value, 'dev', [(i, i ^ bit) for i in range(devices)])  37 us
    pallas_call x1, Pallas kernels, mlp_all(): pl.pallas_call(mlp_kernel, out_shape=(total, total, jax.ShapeDtypeStruct(...  29.7 us
    all_to_all x2, waiting for transfers between devices, in_plane(): lax.all_to_all(stack, 'dev', 0, 0, axis_index_groups=groups_of(devices),...  28.3 us
    all_to_all x1, blocking collectives, across_planes(): lax.all_to_all(stack, 'dev', 0, 0, axis_index_groups=columns, tiled=True)  26.2 us
  transfers between devices with their start and end apart: 27, of which 17 were waited for; matrix products, arithmetic and copies ran while one was open for 15% of the time, Pallas kernels for 21%

profile of v3, /device:TPU:0, one launch (start us, length us, event | category | flops | bytes accessed | tf_op | source)
XLA Modules:
  0.0 601.8 jit_solution(5055657768342288811)
XLA Ops:
  11.7 3.0 collective-permute-start.3
  16.2 7.6 %collective-permute-done.3 = bf16[384,512]{1,0:T(8,128)(2,1)S(1)} collective-permute-done((bf16[384,512]{1,0:T(8,128)(2,1)S(1)}, bf16[384,512]{1,0:T(8,128)(2,1)S(1)}, u32[]{:S(2)}, u32[]{:S(2)}) %collective-permute-start.3) | collective-permute-done | bytes 393248 | tf_op jit(solution)/shard_map/ppermute | solution.py:283
  27.4 19.5 %collective-permute-done.4 = bf16[2,384,512]{2,1,0:T(8,128)(2,1)S(1)} collective-permute-done((bf16[2,384,512]{2,1,0:T(8,128)(2,1)S(1)}, bf16[2,384,512]{2,1,0:T(8,128)(2,1)S(1)}, u32[]{:S(2)}, u32[]{:S(2)}) %collective-permute-start.4) | collective-permute-done | bytes 786464 | tf_op jit(solution)/shard_map/ppermute | solution.py:283
  50.3 4.7 all-to-all-start
  56.0 6.6 %all-to-all-done = bf16[32,2,224]{2,1,0:T(2,128)(2,1)S(1)} async-done(((bf16[32,2,224]{2,1,0:T(2,128)(2,1)}), bf16[32,2,224]{2,1,0:T(2,128)(2,1)S(1)}, u32[]{:S(2)}, u32[]{:S(2)}) %all-to-all-start) | async-done | bytes 28704 | tf_op jit(solution)/shard_map/all_to_all | solution.py:491
  62.6 9.5 %all_to_all.55 = bf16[8,32,384]{2,1,0:T(8,128)(2,1)S(1)} all-to-all(bf16[8,32,384]{2,1,0:T(8,128)(2,1)} %reshape.351), channel_id=1, replica_groups={{0,1,2,3,4,5,6,7},{8,9,10,11,12,13,14,15},{16,17,18,19,20,21,22,23},{24..., dimensions={0} | all-to-all | bytes 393216 | tf_op jit(solution)/shard_map/all_to_all | solution.py:292
  73.1 4.2 all-to-all-start.2
  78.5 39.9 %all-to-all-done.2 = bf16[4,256,384]{2,1,0:T(8,128)(2,1)} async-done(((bf16[4,256,384]{2,1,0:T(8,128)(2,1)}), bf16[4,256,384]{2,1,0:T(8,128)(2,1)}, u32[]{:S(2)}, u32[]{:S(2)}) %all-to-all-start.2) | async-done | bytes 786464 | tf_op jit(solution)/shard_map/all_to_all | solution.py:288
  118.4 11.2 %plane_qkv.1 = (bf16[3072,1024]{1,0:T(8,128)(2,1)}, bf16[3072,128]{1,0:T(8,128)(2,1)S(1)}, bf16[3072,128]{1,0:T(8,128)(2,1)S(1)}, bf16[3072,128]{1,0:T(8,128)(2,1)S(1)}) custom-call(s32[3]{0:T(128)S(1)} %pad_add_fusion.1.bits, bf16[2,2,384,512]{3,2,1,0:T(8,128)(2,1)S(1)} %pad_maximum_fusion.5.near_a, bf16[2,2,384,512]{3,2,1,0:T(8,128)(2,1)} %collective-permute-done.2.far_a, ...), custom_call_target="tpu_custom_call" | custom-call | flops 8053063680 | bytes 16777216 | tf_op jit(solution)/shard_map/plane_qkv/pallas_call | solution.py:339
  134.1 23.8 %collective-permute-done.6 = bf16[1536,256]{1,0:T(8,128)(2,1)S(1)} collective-permute-done((bf16[1536,256]{1,0:T(8,128)(2,1)}, bf16[1536,256]{1,0:T(8,128)(2,1)S(1)}, u32[]{:S(2)}, u32[]{:S(2)}) %collective-permute-start.6) | collective-permute-done | bytes 786464 | tf_op jit(solution)/shard_map/ppermute | solution.py:275
  157.9 4.2 collective-permute-done.7
  164.8 51.8 %attention_forward.1 = (bf16[3072,128]{1,0:T(8,128)(2,1)}, f32[8,3072]{1,0:T(8,128)S(1)}) custom-call(s32[12]{0:T(128)S(1)} %get-tuple-element.160.low, s32[12]{0:T(128)S(1)} %get-tuple-element.161.high, s32[2,3072]{1,0:T(2,128)S(1)} %pad_add_fusion.seg, bf16[3072,128]{1,0:T(8,128)(2,1)S(1)} %copy-done.3, bf16[6144,128]{1,0:T(8,128)(2,1)S(1)} %get-tuple-element.110.k_ref, ...), custom_call_target="tpu_custom_call" | custom-call | flops 9663676416 | bytes 8388608 | tf_op jit(solution)/shard_map/attention_forward/pallas_call | solution.py:140
  216.6 4.4 all-to-all-start.3
  223.1 10.4 %all-to-all-done.3 = bf16[8,384,1,128]{3,1,2,0:T(8,128)(2,1)} async-done(((bf16[8,384,1,128]{3,1,2,0:T(8,128)(2,1)}), bf16[8,384,1,128]{3,1,2,0:T(8,128)(2,1)}, u32[]{:S(2)}, u32[]{:S(2)}) %all-to-all-start.3) | async-done | bytes 786464 | tf_op jit(solution)/shard_map/all_to_all | solution.py:269
  233.6 4.9 fusion.41
  239.2 29.7 %mlp_all.1 = (f32[384,1024]{1,0:T(8,128)}, f32[384,1024]{1,0:T(8,128)}, f32[1,4096]{1,0:T(1,128)S(1)}, bf16[16,32,4096]{2,1,0:T(8,128)(2,1)}, bf16[16,32,4096]{2...) custom-call(s32[3]{0:T(128)S(1)} %pad_add_fusion.1.bits, ...), custom_call_target="tpu_custom_call" | custom-call | flops 19327352832 | bytes 33554432 | tf_op jit(solution)/shard_map/mlp_all/pallas_call | solution.py:418
  271.0 2.7 multiply_reduce_fusion
  273.6 4.2 fusion.24
  280.3 2.8 fusion.28
  285.1 4.2 constant_dynamic-slice_fusion
  289.3 2.4 fusion.3
  298.2 3.8 all-to-all-start.4
  302.0 2.0 collective-permute-start.11
  305.5 3.8 fusion.4
  309.3 3.7 fusion.5
  315.0 60.9 %attention_backward.1 = (bf16[3072,128]{1,0:T(8,128)(2,1)S(1)}, f32[3072,256]{1,0:T(8,128)}, bf16[2,1536,256]{2,1,0:T(8,128)(2,1)S(1)}) custom-call(s32[12]{0:T(128)S(1)} %get-tuple-element.160.low, s32[12]{0:T(128)S(1)} %get-tuple-element.161.high, s32[2,3072]{1,0:T(2,128)S(1)} %pad_add_fusion.seg, bf16[3072,128]{1,0:T(8,128)(2,1)S(1)} %copy-done.4, ...), custom_call_target="tpu_custom_call" | custom-call | flops 24159191040 | bytes 16777216 | tf_op jit(solution)/shard_map/attention_backward/pallas_call | solution.py:165
  376.0 5.2 collective-permute-done.11
  381.2 2.3 add_convert_fusion
  384.1 14.7 %collective-permute-start.13 = (bf16[1536,256]{1,0:T(8,128)(2,1)S(1)}, bf16[1536,256]{1,0:T(8,128)(2,1)S(1)}, u32[]{:S(2)}, u32[]{:S(2)}) collective-permute-start(bf16[1536,256]{1,0:T(8,128)(2,1)S(1)} %get-tuple-element.115), channel_id=1, source_target_pairs={{0,8},{1,9},{2,10},{3,11},{4,12},{5,13},{6,14},{7,15},{8,16},{9,17... | collective-permute-start | bytes 2359304 | tf_op jit(solution)/shard_map/ppermute | solution.py:275
  400.2 2.5 add_convert_fusion.1
  403.8 8.9 %collective-permute-done.13 = bf16[1536,256]{1,0:T(8,128)(2,1)S(1)} collective-permute-done((bf16[1536,256]{1,0:T(8,128)(2,1)S(1)}, bf16[1536,256]{1,0:T(8,128)(2,1)S(1)}, u32[]{:S(2)}, u32[]{:S(2)}) %collective-permute-start.13) | collective-permute-done | bytes 786464 | tf_op jit(solution)/shard_map/ppermute | solution.py:275
  412.8 9.3 %collective-permute-done.14 = bf16[1536,256]{1,0:T(8,128)(2,1)S(1)} collective-permute-done((bf16[1536,256]{1,0:T(8,128)(2,1)S(1)}, bf16[1536,256]{1,0:T(8,128)(2,1)S(1)}, u32[]{:S(2)}, u32[]{:S(2)}) %collective-permute-start.14) | collective-permute-done | bytes 786464 | tf_op jit(solution)/shard_map/ppermute | solution.py:275
  422.9 4.5 collective-permute-done.15
  427.4 3.5 convolution_convert_fusion
  430.9 26.2 %all_to_all.56 = bf16[4,8,32,384]{3,2,1,0:T(8,128)(2,1)S(1)} all-to-all(bf16[4,8,32,384]{3,2,1,0:T(8,128)(2,1)S(1)} %bitcast.211), channel_id=1, replica_groups={{0,8,16,24},{1,9,17,25},{2,10,18,26},{3,11,19,27},{4,12,20,28},{5,13,21..., dimensions={0} | all-to-all | bytes 1572864 | tf_op jit(solution)/shard_map/all_to_all | solution.py:288
  457.9 4.1 all-to-all-start.8
  464.0 4.3 copy.123
  468.2 2.2 all-to-all-done.8
  470.4 4.4 all-to-all-start.5
  478.1 26.1 %all-to-all-done.5 = bf16[8,384,384]{1,2,0:T(8,128)(2,1)} async-done(((bf16[8,384,384]{1,2,0:T(8,128)(2,1)}), bf16[8,384,384]{1,2,0:T(8,128)(2,1)}, u32[]{:S(2)}, u32[]{:S(2)}) %all-to-all-start.5) | async-done | bytes 2359328 | tf_op jit(solution)/shard_map/all_to_all | solution.py:292
  504.2 3.9 all-to-all-start.9
  522.1 37.1 %all-to-all-done.9 = bf16[4,32,9216]{2,1,0:T(8,128)(2,1)S(1)} async-done(((bf16[4,32,9216]{2,1,0:T(8,128)(2,1)}), bf16[4,32,9216]{2,1,0:T(8,128)(2,1)S(1)}, u32[]{:S(2)}, u32[]{:S(2)}) %all-to-all-start.9) | async-done | bytes 2359328 | tf_op jit(solution)/shard_map/all_to_all | solution.py:288
  562.3 3.1 copy.163
  565.5 4.5 reshape.388
  571.7 7.7 %fusion.22 = (f32[1024]{0:T(1024)S(1)}, f32[384]{0:T(512)S(1)}, f32[384]{0:T(512)S(1)}, f32[1024]{0:T(1024)S(1)}, f32[384,1024]{1,0:T(8,128)}) fusion(bf16[384,1024]{1,0:T(8,128)(2,1)S(1)} %copy-done.15, f32[384]{0:T(512)S(1)} %copy-done.51, f32[384]{0:T(512)S(1)} %copy-done.49, f32[1024]{0:T(1024)S(1)} %copy-done.46, bf16[384,3072]{0,1:T(8,128)(2,1)} %bitcast.193, ...), kind=kOutput, calls=%fused_computation.44 | convolution fusion | flops 2419848192 | bytes 11028480 | tf_op jit(solution)/shard_map/tf,df->td/dot_general | solution.py:209
  580.4 5.0 all-to-all-start.6
  585.4 2.9 fusion.21
  588.3 4.5 all-to-all-done.6
  (290 shorter events, 73.1 us)
Async XLA Ops:
  7.2 226.4 %all-gather.3.cloned.1.call-start = ((), (), s32[]{:S(2)}) async-start(), calls=%async_computation.10 | async-start | bytes 19464192 | tf_op jit(solution)/shard_map/all_gather | solution.py:239
  11.7 12.1 %collective-permute-start.3 = (bf16[384,512]{1,0:T(8,128)(2,1)S(1)}, bf16[384,512]{1,0:T(8,128)(2,1)S(1)}, u32[]{:S(2)}, u32[]{:S(2)}) collective-permute-start(bf16[384,512]{1,0:T(8,128)(2,1)S(1)} %get-tuple-element.136), channel_id=1, source_target_pairs={{0,2},{1,3},{2,0},{3,1},{4,6},{5,7},{6,4},{7,5},{8,10},{9,11},{10,... | collective-permute-start | bytes 1179656 | tf_op jit(solution)/shard_map/ppermute | solution.py:283
  14.7 11.1 %collective-permute-start = (bf16[384,512]{1,0:T(8,128)(2,1)S(1)}, bf16[384,512]{1,0:T(8,128)(2,1)S(1)}, u32[]{:S(2)}, u32[]{:S(2)}) collective-permute-start(bf16[384,512]{1,0:T(8,128)(2,1)S(1)} %get-tuple-element.137), channel_id=1, source_target_pairs={{0,4},{1,5},{2,6},{3,7},{4,0},{5,1},{6,2},{7,3},{8,12},{9,13},{10,... | collective-permute-start | bytes 1179656 | tf_op jit(solution)/shard_map/ppermute | solution.py:283
  23.9 23.0 %collective-permute-start.4 = (bf16[2,384,512]{2,1,0:T(8,128)(2,1)S(1)}, bf16[2,384,512]{2,1,0:T(8,128)(2,1)S(1)}, u32[]{:S(2)}, u32[]{:S(2)}) collective-permute-start(bf16[2,384,512]{2,1,0:T(8,128)(2,1)S(1)} %get-tuple-element.133), channel_id=1, source_target_pairs={{0,4},{1,5},{2,6},{3,7},{4,0},{5,1},{6,2},{7,3},{8,12},{9,13},{10,... | collective-permute-start | bytes 2359304 | tf_op jit(solution)/shard_map/ppermute | solution.py:283
  25.9 21.4 %collective-permute-start.1 = (bf16[2,384,512]{2,1,0:T(8,128)(2,1)S(1)}, bf16[2,384,512]{2,1,0:T(8,128)(2,1)S(1)}, u32[]{:S(2)}, u32[]{:S(2)}) collective-permute-start(bf16[2,384,512]{2,1,0:T(8,128)(2,1)S(1)} %get-tuple-element.139), channel_id=1, source_target_pairs={{0,2},{1,3},{2,0},{3,1},{4,6},{5,7},{6,4},{7,5},{8,10},{9,11},{10,... | collective-permute-start | bytes 2359304 | tf_op jit(solution)/shard_map/ppermute | solution.py:283
  47.2 71.1 %collective-permute-start.5 = (bf16[2,2,384,512]{3,2,1,0:T(8,128)(2,1)S(1)}, bf16[2,2,384,512]{3,2,1,0:T(8,128)(2,1)}, u32[]{:S(2)}, u32[]{:S(2)}) collective-permute-start(bf16[2,2,384,512]{3,2,1,0:T(8,128)(2,1)S(1)} %pad_maximum_fusion.6.near_b), channel_id=1, source_target_pairs={{0,1},{1,0},{2,3},{3,2},{4,5},{5,4},{6,7},{7,6},{8,9},{9,8},{10,11... | collective-permute-start | bytes 4718600 | tf_op jit(solution)/shard_map/ppermute | solution.py:283
  47.5 70.9 %collective-permute-start.2 = (bf16[2,2,384,512]{3,2,1,0:T(8,128)(2,1)S(1)}, bf16[2,2,384,512]{3,2,1,0:T(8,128)(2,1)}, u32[]{:S(2)}, u32[]{:S(2)}) collective-permute-start(bf16[2,2,384,512]{3,2,1,0:T(8,128)(2,1)S(1)} %pad_maximum_fusion.5.near_a), channel_id=1, source_target_pairs={{0,1},{1,0},{2,3},{3,2},{4,5},{5,4},{6,7},{7,6},{8,9},{9,8},{10,11... | collective-permute-start | bytes 4718600 | tf_op jit(solution)/shard_map/ppermute | solution.py:283
  50.3 12.3 %all-to-all-start = ((bf16[32,2,224]{2,1,0:T(2,128)(2,1)}), bf16[32,2,224]{2,1,0:T(2,128)(2,1)S(1)}, u32[]{:S(2)}, u32[]{:S(2)}) async-start(bf16[32,2,224]{2,1,0:T(2,128)(2,1)} %reshape.407), calls=%async_computation | async-start | bytes 65536 | tf_op jit(solution)/shard_map/all_to_all | solution.py:491
  55.1 22.3 %copy-start.64 = (s32[12]{0:T(128)S(1)}, s32[12]{0:T(128)}, u32[]{:S(2)}) copy-start(s32[12]{0:T(128)} %param.19) | copy-start | bytes 148
  73.1 45.3 %all-to-all-start.2 = ((bf16[4,256,384]{2,1,0:T(8,128)(2,1)}), bf16[4,256,384]{2,1,0:T(8,128)(2,1)}, u32[]{:S(2)}, u32[]{:S(2)}) async-start(bf16[4,256,384]{2,1,0:T(8,128)(2,1)} %broadcast_in_dim.36), calls=%async_computation.2 | async-start | bytes 1572864 | tf_op jit(solution)/shard_map/all_to_all | solution.py:288
  78.3 51.3 %copy-start.29 = (f32[32,32]{1,0:T(8,128)}, f32[32,32]{1,0:T(8,128)S(1)}, u32[]{:S(2)}) copy-start(f32[32,32]{1,0:T(8,128)S(1)} %get-tuple-element.146) | copy-start | bytes 12292
  131.2 26.8 %collective-permute-start.6 = (bf16[1536,256]{1,0:T(8,128)(2,1)}, bf16[1536,256]{1,0:T(8,128)(2,1)S(1)}, u32[]{:S(2)}, u32[]{:S(2)}) collective-permute-start(bf16[1536,256]{1,0:T(8,128)(2,1)} %get-tuple-element.117), channel_id=1, source_target_pairs={{0,8},{1,9},{2,10},{3,11},{4,12},{5,13},{6,14},{7,15},{8,16},{9,17... | collective-permute-start | bytes 2359304 | tf_op jit(solution)/shard_map/ppermute | solution.py:275
  132.5 29.6 %collective-permute-start.7 = (bf16[1536,256]{1,0:T(8,128)(2,1)}, bf16[1536,256]{1,0:T(8,128)(2,1)}, u32[]{:S(2)}, u32[]{:S(2)}) collective-permute-start(bf16[1536,256]{1,0:T(8,128)(2,1)} %get-tuple-element.118), channel_id=1, source_target_pairs={{8,0},{9,1},{10,2},{11,3},{12,4},{13,5},{14,6},{15,7},{16,8},{17,9... | collective-permute-start | bytes 2359304 | tf_op jit(solution)/shard_map/ppermute | solution.py:275
  163.9 52.7 %copy-start = (bf16[6144,128]{1,0:T(8,128)(2,1)}, bf16[6144,128]{1,0:T(8,128)(2,1)S(1)}, u32[]{:S(2)}) copy-start(bf16[6144,128]{1,0:T(8,128)(2,1)S(1)} %get-tuple-element.109.v_ref) | copy-start | bytes 4718596
  163.9 52.7 %copy-start.1 = (bf16[6144,128]{1,0:T(8,128)(2,1)}, bf16[6144,128]{1,0:T(8,128)(2,1)S(1)}, u32[]{:S(2)}) copy-start(bf16[6144,128]{1,0:T(8,128)(2,1)S(1)} %get-tuple-element.110.k_ref) | copy-start | bytes 4718596
  216.6 17.0 %all-to-all-start.3 = ((bf16[8,384,1,128]{3,1,2,0:T(8,128)(2,1)}), bf16[8,384,1,128]{3,1,2,0:T(8,128)(2,1)}, u32[]{:S(2)}, u32[]{:S(2)}) async-start(bf16[8,384,1,128]{3,1,2,0:T(8,128)(2,1)} %bitcast.31), calls=%async_computation.3 | async-start | bytes 1572864 | tf_op jit(solution)/shard_map/all_to_all | solution.py:269
  221.0 350.6 %all-gather.5.cloned.1.call-start = ((), (), s32[]{:S(2)}) async-start(), calls=%async_computation.11 | async-start | bytes 6488064 | tf_op jit(solution)/shard_map/all_gather | solution.py:239
  221.2 17.3 %copy-start.48 = (f32[384]{0:T(512)}, f32[384]{0:T(512)S(1)}, u32[]{:S(2)}) copy-start(f32[384]{0:T(512)S(1)} %broadcast_multiply_fusion.2) | copy-start | bytes 4612
  238.5 30.4 %copy-start.5 = (f32[384,1024]{1,0:T(8,128)}, f32[384,1024]{1,0:T(8,128)S(1)}, u32[]{:S(2)}) copy-start(f32[384,1024]{1,0:T(8,128)S(1)} %get-tuple-element.104) | copy-start | bytes 4718596
  268.9 14.9 %collective-permute-start.8 = (bf16[16,32,4096]{2,1,0:T(8,128)(2,1)}, bf16[16,32,4096]{2,1,0:T(8,128)(2,1)}, u32[]{:S(2)}, u32[]{:S(2)}) collective-permute-start(bf16[16,32,4096]{2,1,0:T(8,128)(2,1)} %get-tuple-element.58), channel_id=1, source_target_pairs={{0,1},{1,0},{2,3},{3,2},{4,5},{5,4},{6,7},{7,6},{8,9},{9,8},{10,11... | collective-permute-start | bytes 12582920 | tf_op jit(solution)/shard_map/ppermute | solution.py:283
  269.0 14.8 %collective-permute-start.9 = (bf16[16,32,4096]{2,1,0:T(8,128)(2,1)}, bf16[16,32,4096]{2,1,0:T(8,128)(2,1)}, u32[]{:S(2)}, u32[]{:S(2)}) collective-permute-start(bf16[16,32,4096]{2,1,0:T(8,128)(2,1)} %get-tuple-element.59), channel_id=1, source_target_pairs={{0,1},{1,0},{2,3},{3,2},{4,5},{5,4},{6,7},{7,6},{8,9},{9,8},{10,11... | collective-permute-start | bytes 12582920 | tf_op jit(solution)/shard_map/ppermute | solution.py:283
  280.0 3.8 collective-permute-start.10
  298.2 16.8 %all-to-all-start.4 = ((bf16[8,384,1,128]{3,1,2,0:T(8,128)(2,1)}), bf16[8,384,1,128]{3,1,2,0:T(8,128)(2,1)S(1)}, u32[]{:S(2)}, u32[]{:S(2)}) async-start(bf16[8,384,1,128]{3,1,2,0:T(8,128)(2,1)} %bitcast.198), calls=%async_computation.4 | async-start | bytes 1572864 | tf_op jit(solution)/shard_map/all_to_all | solution.py:262
  302.0 79.2 %collective-permute-start.11 = (bf16[4,2,32,4608]{3,2,0,1:T(8,128)(2,1)}, bf16[4,2,32,4608]{3,2,0,1:T(8,128)(2,1)}, u32[]{:S(2)}, u32[]{:S(2)}) collective-permute-start(bf16[4,2,32,4608]{3,2,0,1:T(8,128)(2,1)} %pad_maximum_fusion.1), channel_id=1, source_target_pairs={{0,2},{1,3},{2,0},{3,1},{4,6},{5,7},{6,4},{7,5},{8,10},{9,11},{10,... | collective-permute-start | bytes 7077896 | tf_op jit(solution)/shard_map/ppermute | solution.py:283
  304.0 77.1 %collective-permute-start.12 = (bf16[4,2,32,4608]{3,2,1,0:T(8,128)(2,1)}, bf16[4,2,32,4608]{3,2,1,0:T(8,128)(2,1)}, u32[]{:S(2)}, u32[]{:S(2)}) collective-permute-start(bf16[4,2,32,4608]{3,2,1,0:T(8,128)(2,1)} %pad_maximum_fusion.2), channel_id=1, source_target_pairs={{0,4},{1,5},{2,6},{3,7},{4,0},{5,1},{6,2},{7,3},{8,12},{9,13},{10,... | collective-permute-start | bytes 7077896 | tf_op jit(solution)/shard_map/ppermute | solution.py:283
  315.0 66.1 %copy-start.12 = (bf16[4,2,32,4096]{3,2,1,0:T(8,128)(2,1)S(1)}, bf16[4,2,32,4096]{3,2,1,0:T(8,128)(2,1)}, u32[]{:S(2)}) copy-start(bf16[4,2,32,4096]{3,2,1,0:T(8,128)(2,1)} %fusion.5) | copy-start | bytes 6291460
  315.0 66.1 %copy-start.26 = (bf16[4,2,32,512]{3,2,1,0:T(8,128)(2,1)S(1)}, bf16[4,2,32,512]{3,2,1,0:T(8,128)(2,1)}, u32[]{:S(2)}) copy-start(bf16[4,2,32,512]{3,2,1,0:T(8,128)(2,1)} %get-tuple-element.123) | copy-start | bytes 786436
  383.6 16.6 %copy-start.11 = (bf16[4,2,32,4096]{3,2,0,1:T(8,128)(2,1)S(1)}, bf16[4,2,32,4096]{3,2,0,1:T(8,128)(2,1)}, u32[]{:S(2)}) copy-start(bf16[4,2,32,4096]{3,2,0,1:T(8,128)(2,1)} %fusion.4) | copy-start | bytes 6291460
  383.6 39.3 %collective-permute-start.16 = (bf16[4,32,4608]{2,1,0:T(8,128)(2,1)S(1)}, bf16[4,32,4608]{2,1,0:T(8,128)(2,1)S(1)}, u32[]{:S(2)}, u32[]{:S(2)}) collective-permute-start(bf16[4,32,4608]{2,1,0:T(8,128)(2,1)S(1)} %dynamic-slice_bitcast_fusion), channel_id=1, source_target_pairs={{0,2},{1,3},{2,0},{3,1},{4,6},{5,7},{6,4},{7,5},{8,10},{9,11},{10,... | collective-permute-start | bytes 3538952 | tf_op jit(solution)/shard_map/ppermute | solution.py:283
  384.1 28.7 %collective-permute-start.13 = (bf16[1536,256]{1,0:T(8,128)(2,1)S(1)}, bf16[1536,256]{1,0:T(8,128)(2,1)S(1)}, u32[]{:S(2)}, u32[]{:S(2)}) collective-permute-start(bf16[1536,256]{1,0:T(8,128)(2,1)S(1)} %get-tuple-element.115), channel_id=1, source_target_pairs={{0,8},{1,9},{2,10},{3,11},{4,12},{5,13},{6,14},{7,15},{8,16},{9,17... | collective-permute-start | bytes 2359304 | tf_op jit(solution)/shard_map/ppermute | solution.py:275
  398.8 23.2 %collective-permute-start.14 = (bf16[1536,256]{1,0:T(8,128)(2,1)S(1)}, bf16[1536,256]{1,0:T(8,128)(2,1)S(1)}, u32[]{:S(2)}, u32[]{:S(2)}) collective-permute-start(bf16[1536,256]{1,0:T(8,128)(2,1)S(1)} %get-tuple-element.116), channel_id=1, source_target_pairs={{8,0},{9,1},{10,2},{11,3},{12,4},{13,5},{14,6},{15,7},{16,8},{17,9... | collective-permute-start | bytes 2359304 | tf_op jit(solution)/shard_map/ppermute | solution.py:275
  400.2 21.9 %copy-start.21 = (f32[3072,256]{1,0:T(8,128)S(1)}, f32[3072,256]{1,0:T(8,128)}, u32[]{:S(2)}) copy-start(f32[3072,256]{1,0:T(8,128)} %get-tuple-element.76) | copy-start | bytes 9437188
  400.2 27.3 %slice-start = ((s8[6291456]{0:T(1024)(128)(4,1)}), s8[4194304]{0:T(1024)(128)(4,1)S(1)}, s32[]{:S(2)}) async-start(s8[6291456]{0:T(1024)(128)(4,1)} %bitcast.243), calls=%async_computation.12 | async-start | bytes 8388608
  402.6 19.9 %copy-start.9 = (bf16[4,2,32,4608]{3,2,0,1:T(8,128)(2,1)}, bf16[4,2,32,4608]{3,2,0,1:T(8,128)(2,1)S(1)}, u32[]{:S(2)}) copy-start(bf16[4,2,32,4608]{3,2,0,1:T(8,128)(2,1)S(1)} %add_convert_fusion.1) | copy-start | bytes 7077892
  402.7 24.7 %slice-start.1 = ((s8[6291456]{0:T(1024)(128)(4,1)}), s8[2097152]{0:T(1024)(128)(4,1)S(1)}, s32[]{:S(2)}) async-start(s8[6291456]{0:T(1024)(128)(4,1)} %bitcast.243), calls=%async_computation.13 | async-start | bytes 4194304
  402.8 24.7 %collective-permute-start.15 = (bf16[4,32,4608]{2,1,0:T(8,128)(2,1)S(1)}, bf16[4,32,4608]{2,1,0:T(8,128)(2,1)S(1)}, u32[]{:S(2)}, u32[]{:S(2)}) collective-permute-start(bf16[4,32,4608]{2,1,0:T(8,128)(2,1)S(1)} %dynamic-slice_bitcast_fusion.1), channel_id=1, source_target_pairs={{0,4},{1,5},{2,6},{3,7},{4,0},{5,1},{6,2},{7,3},{8,12},{9,13},{10,... | collective-permute-start | bytes 3538952 | tf_op jit(solution)/shard_map/ppermute | solution.py:283
  457.9 12.5 %all-to-all-start.8 = ((f32[8,32,384]{2,1,0:T(8,128)}), f32[8,32,384]{2,1,0:T(8,128)}, u32[]{:S(2)}, u32[]{:S(2)}) async-start(f32[8,32,384]{2,1,0:T(8,128)} %convert_reduce_fusion.2), calls=%async_computation.8 | async-start | bytes 786432 | tf_op jit(solution)/shard_map/all_to_all | solution.py:292
  470.4 33.8 %all-to-all-start.5 = ((bf16[8,384,384]{1,2,0:T(8,128)(2,1)}), bf16[8,384,384]{1,2,0:T(8,128)(2,1)}, u32[]{:S(2)}, u32[]{:S(2)}) async-start(bf16[8,384,384]{1,2,0:T(8,128)(2,1)} %copy.123), calls=%async_computation.5 | async-start | bytes 4718592 | tf_op jit(solution)/shard_map/all_to_all | solution.py:292
  478.1 30.1 %copy-start.30 = (f32[32,32]{1,0:T(8,128)S(1)}, f32[32,32]{1,0:T(8,128)}, u32[]{:S(2)}) copy-start(f32[32,32]{1,0:T(8,128)} %copy-done.29) | copy-start | bytes 12292
  478.1 30.7 %copy-start.45 = (f32[1024]{0:T(1024)S(1)}, f32[1024]{0:T(1024)}, u32[]{:S(2)}) copy-start(f32[1024]{0:T(1024)} %get-tuple-element.112) | copy-start | bytes 12292
  478.1 31.4 %copy-start.44 = (f32[1024]{0:T(1024)S(1)}, f32[1024]{0:T(1024)}, u32[]{:S(2)}) copy-start(f32[1024]{0:T(1024)} %get-tuple-element.113) | copy-start | bytes 12292
  478.1 32.1 %copy-start.43 = (f32[1024]{0:T(1024)S(1)}, f32[1024]{0:T(1024)}, u32[]{:S(2)}) copy-start(f32[1024]{0:T(1024)} %get-tuple-element.99) | copy-start | bytes 12292
  478.1 32.7 %copy-start.42 = (f32[1024]{0:T(1024)S(1)}, f32[1024]{0:T(1024)}, u32[]{:S(2)}) copy-start(f32[1024]{0:T(1024)} %get-tuple-element.98) | copy-start | bytes 12292
  478.1 35.4 %copy-start.41 = (f32[1024]{0:T(1024)S(1)}, f32[1024]{0:T(1024)}, u32[]{:S(2)}) copy-start(f32[1024]{0:T(1024)} %get-tuple-element.86) | copy-start | bytes 12292
  478.1 36.1 %copy-start.40 = (f32[1024]{0:T(1024)S(1)}, f32[1024]{0:T(1024)}, u32[]{:S(2)}) copy-start(f32[1024]{0:T(1024)} %get-tuple-element.94) | copy-start | bytes 12292
  478.1 36.8 %copy-start.53 = (f32[384]{0:T(512)S(1)}, f32[384]{0:T(512)}, u32[]{:S(2)}) copy-start(f32[384]{0:T(512)} %get-tuple-element.131) | copy-start | bytes 4612
  504.2 55.0 %all-to-all-start.9 = ((bf16[4,32,9216]{2,1,0:T(8,128)(2,1)}), bf16[4,32,9216]{2,1,0:T(8,128)(2,1)S(1)}, u32[]{:S(2)}, u32[]{:S(2)}) async-start(bf16[4,32,9216]{2,1,0:T(8,128)(2,1)} %pad_maximum_fusion.4), calls=%async_computation.9 | async-start | bytes 4718592 | tf_op jit(solution)/shard_map/all_to_all | solution.py:288
  580.4 12.4 %all-to-all-start.6 = ((f32[32,1,448]{2,1,0:T(1,128)}), f32[32,1,448]{2,1,0:T(1,128)S(1)}, u32[]{:S(2)}, u32[]{:S(2)}) async-start(f32[32,1,448]{2,1,0:T(1,128)} %copy.126), calls=%async_computation.6 | async-start | bytes 131072 | tf_op jit(solution)/shard_map/all_to_all | solution.py:642
  (46 other events, 230.2 us)
Sparse Core Ops, SparseCore 0:
  11.7 149.0 all-gather.2
  280.2 91.8 all-gather.4
